TPU v7x, 256 devices: a whole 4x4x8 slice. The times are simulated.
256 devices in a mesh: dp: 32 (over y, x, core), head: 8 (over z).
Axes of the slice: x: 4, y: 4, z: 8, core: 2. Of those that a mesh axis runs over, the one named last changes fastest.
Arguments:
- queries: bfloat16 [32768, 8192], P(('dp', 'head')), may hold values from -80 to 80
- input_keys: bfloat16 [32768, 1024], P(('dp', 'head')), may hold values from -4 to 4
- input_values: bfloat16 [32768, 1024], P(('dp', 'head')), may hold values from -6 to 6
- output_gradient: bfloat16 [32768, 8192], P(('dp', 'head')), may hold values from -6 to 6
- doc_ids: int32 [32768], P('dp'), may hold values from 0 to 63, as said below
- spill_src: int32 [32], replicated, may hold values from 0 to 31, as said below
- spill_len: int32 [32], replicated, may hold values from 1 to 128, as said below
Outputs:
- attn_out: bfloat16 [32768, 8192], P(('dp', 'head'))
- grad_queries: bfloat16 [32768, 8192], P(('dp', 'head'))
- grad_keys: bfloat16 [32768, 1024], P(('dp', 'head'))
- grad_values: bfloat16 [32768, 1024], P(('dp', 'head'))
Inputs may be any that keep to these rules, and one draw needn't show every extreme that they name: `doc_ids`: within each bin of 1024 tokens the document numbers start at 0, never fall and rise by at most one from one token to the next; the last document of every bin holds more than 128 tokens; some bin reaches the largest. `spill_src`: every bin is the source of exactly one bin and never its own source. `spill_len`: the value 128 is taken by some bin in every draw.
All inputs are finite; a program needn't handle non-finite values.
Results may differ from a plain program's by a relative error of at most 0.04.
Values may be sent and summed in bfloat16 or wider, within the bound.
No kernel may reach another device: no remote copies, remote signals or barrier semaphores. Data moves between devices by JAX's collectives and lax.ppermute only.
A program may use at most 192 MiB of HBM per device.

v0:
```python
import functools

import jax
import jax.numpy as jnp
from jax import lax
from jax.experimental import pallas as pl
from jax.experimental.pallas import tpu as pltpu
from jax.sharding import PartitionSpec as P

HEAD = 128
GROUP = 8
KV_HEADS = 8
ROWS = 128
WIDE = GROUP * ROWS
TAIL = 128
KEYS = 1024 + TAIL
PAIR = 256
LOG2E = 1.4426950408889634
SCALE = HEAD**-0.5
MASKED = -1e30
F32 = jnp.float32
BF16 = jnp.bfloat16
NT = (((1,), (1,)), ((), ()))
TN = (((0,), (0,)), ((), ()))
CHUNKS = [(0, 128)] + [(128 + 256 * i, 256) for i in range(4)]


def dot(a, b, dims=(((1,), (0,)), ((), ()))):
    return lax.dot_general(a, b, dims, preferred_element_type=F32)


def fold(x, op):
    return op(x.reshape(x.shape[0] // 8, 8, x.shape[1]), axis=0)


def body(bias, q_ref, do_ref, near, far, o_ref, dq_ref, dnear, dfar, s_ref, p_ref, dk_ref, dv_ref):
    keys, values = [far[0]], [far[1]]
    for i in range(4):
        keys.append(near[2 * i : 2 * i + 2, 0].reshape(PAIR, HEAD))
        values.append(near[2 * i : 2 * i + 2, 1].reshape(PAIR, HEAD))
    for pair in range(GROUP // 2):
        cut = [slice((2 * pair + h) * HEAD, (2 * pair + h + 1) * HEAD) for h in range(2)]
        q2 = jnp.concatenate([q_ref[:, at] for at in cut], axis=0)
        do2 = jnp.concatenate([do_ref[:, at] for at in cut], axis=0)
        dot2 = jnp.concatenate([do_ref[:, at].T for at in cut], axis=1)
        high = None
        for c, (at, size) in enumerate(CHUNKS):
            mask = bias[at : at + size]
            s = dot(keys[c], q2, NT) * (SCALE * LOG2E) + jnp.concatenate([mask, mask], axis=1)
            s_ref[pair, at : at + size] = s
            top = fold(s, jnp.max)
            high = top if high is None else jnp.maximum(high, top)
        high = jnp.max(high, axis=0, keepdims=True)
        norm = 0.0
        for c, (at, size) in enumerate(CHUNKS):
            p = jnp.exp2(s_ref[pair, at : at + size] - high)
            s_ref[pair, at : at + size] = p
            norm = norm + fold(p, jnp.sum)
        scale = 1.0 / jnp.sum(norm, axis=0, keepdims=True)
        out = 0.0
        for c, (at, size) in enumerate(CHUNKS):
            w = s_ref[pair, at : at + size] * scale
            w16 = w.astype(BF16)
            p_ref[pair, at : at + size] = w16
            out = out + dot(values[c], w16, TN)
        out = out.astype(BF16)
        for h in range(2):
            o_ref[:, cut[h]] = out[:, h * HEAD : (h + 1) * HEAD].T
        delta = jnp.sum(dot2.astype(F32) * out.astype(F32), axis=0, keepdims=True)
        grad = 0.0
        for c, (at, size) in enumerate(CHUNKS):
            w16 = p_ref[pair, at : at + size]
            ds = (w16.astype(F32) * (dot(values[c], dot2) - delta)).astype(BF16)
            dv = dot(w16, do2)
            dk = dot(ds, q2)
            if pair:
                dv_ref[at : at + size] += dv
                dk_ref[at : at + size] += dk
            else:
                dv_ref[at : at + size] = dv
                dk_ref[at : at + size] = dk
            grad = grad + dot(keys[c], ds, TN)
        grad = (grad * SCALE).astype(BF16)
        for h in range(2):
            dq_ref[:, cut[h]] = grad[:, h * HEAD : (h + 1) * HEAD].T
    dk = (dk_ref[...] * SCALE).astype(BF16)
    dv = dv_ref[...].astype(BF16)
    dfar[0], dfar[1] = dk[:TAIL], dv[:TAIL]
    for i in range(8):
        at = slice(TAIL + i * ROWS, TAIL + (i + 1) * ROWS)
        dnear[i, 0], dnear[i, 1] = dk[at], dv[at]


def attend(bias, queries, grad, near, far):
    wide = pl.BlockSpec((ROWS, WIDE), lambda k: (0, k))
    near_spec = pl.BlockSpec((8, 2, ROWS, HEAD), lambda k: (0, 0, 0, k))
    far_spec = pl.BlockSpec((2, ROWS, HEAD), lambda k: (0, 0, k))
    return pl.pallas_call(
        body,
        grid=(KV_HEADS,),
        in_specs=[pl.BlockSpec((KEYS, ROWS), lambda k: (0, 0)), wide, wide, near_spec, far_spec],
        out_specs=[wide, wide, near_spec, far_spec],
        out_shape=[jax.ShapeDtypeStruct(a.shape, BF16) for a in (queries, grad, near, far)],
        scratch_shapes=[
            pltpu.VMEM((GROUP // 2, KEYS, PAIR), F32),
            pltpu.VMEM((GROUP // 2, KEYS, PAIR), BF16),
            pltpu.VMEM((KEYS, HEAD), F32),
            pltpu.VMEM((KEYS, HEAD), F32),
        ],
        compiler_params=pltpu.CompilerParams(vmem_limit_bytes=48 * 2**20),
        cost_estimate=pl.CostEstimate(
            flops=6 * 2 * HEAD * KEYS * WIDE * KV_HEADS,
            bytes_accessed=18 * 2**20,
            transcendentals=KEYS * WIDE * KV_HEADS,
        ),
    )(bias, queries, grad, near, far)


def split(block):
    return block.reshape(2, 16, 8, 8, HEAD).transpose(0, 1, 3, 2, 4).reshape(256, 8, HEAD)


def join(pieces):
    return pieces.reshape(2, 16, 8, 8, HEAD).transpose(0, 1, 3, 2, 4).reshape(2, TAIL, 1024)


def exchange(pieces):
    return lax.all_to_all(pieces, ("dp", "head"), split_axis=0, concat_axis=0, tiled=True)


def per_device(queries, input_keys, input_values, output_gradient, doc_ids, spill_src, spill_len):
    rank, z = lax.axis_index("dp"), lax.axis_index("head")
    ids = jnp.arange(32, dtype=jnp.int32)
    kv = jnp.stack([input_keys, input_values])
    near = lax.all_gather(kv, "head", axis=0)

    pieces = exchange(split(kv)).reshape(32, 8, 8 * HEAD)[:, 7]
    wanted = (spill_src[:, None] == ids[None, :]).astype(BF16)
    pieces = jnp.dot(wanted, pieces, preferred_element_type=F32).astype(BF16)
    pieces = jnp.broadcast_to(pieces.reshape(32, 1, 8, HEAD), (32, 8, 8, HEAD)).reshape(256, 8, HEAD)
    far = join(exchange(pieces))

    place = jnp.arange(1024, dtype=jnp.int32)
    row_at = z * ROWS + jnp.arange(ROWS, dtype=jnp.int32)
    row_docs = lax.dynamic_slice_in_dim(doc_ids, z * ROWS, ROWS)
    near_seen = (doc_ids[:, None] == row_docs[None, :]) & (place[:, None] <= row_at[None, :])
    far_seen = (place[:TAIL, None] >= TAIL - spill_len[rank]) & (row_docs[None, :] == 0)
    seen = jnp.concatenate([far_seen, near_seen], axis=0)
    bias = jnp.where(seen, 0.0, MASKED).astype(F32)

    out, dq, dnear, dfar = attend(bias, queries, output_gradient, near, far)

    home = lax.psum_scatter(dnear, "head", scatter_dimension=0)
    pieces = exchange(split(dfar)).reshape(32, 8, 8 * HEAD)
    pieces = jnp.sum(pieces.astype(F32), axis=1).astype(BF16)
    pieces = jnp.dot(wanted.T, pieces, preferred_element_type=F32).astype(BF16)
    pieces = jnp.broadcast_to(pieces.reshape(32, 1, 8, HEAD), (32, 8, 8, HEAD)).reshape(256, 8, HEAD)
    returned = jnp.where(z == 7, join(exchange(pieces)).astype(F32), 0.0)
    total = (home.astype(F32) + returned).astype(BF16)
    return out, dq, total[0], total[1]


def solution(mesh):
    rows = P(("dp", "head"), None)
    return jax.shard_map(
        per_device,
        mesh=mesh,
        in_specs=(rows, rows, rows, rows, P("dp"), P(), P()),
        out_specs=(rows, rows, rows, rows),
        check_vma=False,
    )
```

profile of v0, /device:TPU:1, one launch (start us, length us, event | category | flops | bytes accessed | tf_op | source)
XLA Modules:
  0.0 236.8 jit_solution(5349577219003101255)
XLA Ops:
  7.2 0.0 all-gather.3.cloned.1.call-start
  7.2 1.9 pad_maximum_fusion
  9.1 0.0 copy-start.3
  9.1 0.0 all-gather.3.cloned.1.call-update
  9.1 1.1 pad_maximum_fusion.1
  10.2 0.0 copy-start.4
  10.2 0.0 copy-start.2
  10.2 41.9 %all_to_all.20 = bf16[256,8,128]{2,1,0:T(8,128)(2,1)S(1)} all-to-all(bf16[256,8,128]{2,1,0:T(8,128)(2,1)S(1)} %bitcast.50), channel_id=1, replica_groups=mesh['dp'=32,'head'=8] {'dp','head'}, dimensions={0} | all-to-all | bytes 1048576 | tf_op jit(solution)/shard_map/all_to_all | solution.py:128
  52.1 0.2 reshape.70
  52.3 0.1 slice.16
  52.5 0.0 copy-done.3
  52.5 0.2 fusion
  52.7 0.9 broadcast_in_dim.37
  53.6 5.9 %all-to-all-start.1 = ((bf16[256,8,128]{2,1,0:T(8,128)(2,1)}), bf16[256,8,128]{2,1,0:T(8,128)(2,1)S(1)}, u32[]{:S(2)}, u32[]{:S(2)}) async-start(bf16[256,8,128]{2,1,0:T(8,128)(2,1)} %bitcast.8), calls=%async_computation.1 | async-start | bytes 1048576 | tf_op jit(solution)/shard_map/all_to_all | solution.py:128
  59.5 0.0 reduce-scatter.2.cloned.1.call-start
  59.5 0.0 copy-done.4
  59.5 0.6 dynamic_slice.6
  60.8 0.0 copy-done.2
  60.8 0.1 broadcast_compare_fusion
  60.9 0.1 broadcast_and_fusion
  61.0 0.2 fusion.3
  61.2 0.1 add_select_fusion.bias
  61.3 25.1 %all-to-all-done.1 = bf16[256,8,128]{2,1,0:T(8,128)(2,1)S(1)} async-done(((bf16[256,8,128]{2,1,0:T(8,128)(2,1)}), bf16[256,8,128]{2,1,0:T(8,128)(2,1)S(1)}, u32[]{:S(2)}, u32[]{:S(2)}) %all-to-all-start.1) | async-done | bytes 524320 | tf_op jit(solution)/shard_map/all_to_all | solution.py:128
  86.3 5.3 %all-gather.3.cloned.1.call-done = bf16[16,128,1024]{2,1,0:T(8,128)(2,1)} async-done(((bf16[2,128,1024]{2,1,0:T(8,128)(2,1)}), bf16[16,128,1024]{2,1,0:T(8,128)(2,1)}) %all-gather.3.cloned.1.call-update) | async-done | bytes 4194320 | tf_op jit(solution)/shard_map/all_gather | solution.py:135
  91.6 0.0 copy-start
  91.6 1.6 copy-done
  93.2 0.0 copy-start.1
  93.2 1.6 copy-done.1
  94.8 56.6 %shard_map.102 = (bf16[128,8192]{1,0:T(8,128)(2,1)}, bf16[128,8192]{1,0:T(8,128)(2,1)}, bf16[8,2,128,1024]{3,2,1,0:T(8,128)(2,1)}, bf16[2,128,1024]{2,1,0:T(8,128)(2,1)S(1)}) custom-call(f32[1152,128]{1,0:T(8,128)S(1)} %add_select_fusion.bias, bf16[128,8192]{1,0:T(8,128)(2,1)S(1)} %copy-done, bf16[128,8192]{1,0:T(8,128)(2,1)S(1)} %copy-done.1, ...), custom_call_target="tpu_custom_call" | custom-call | flops 14495514624 | bytes 18874368 | tf_op jit(solution)/shard_map/pallas_call | solution.py:98
  151.4 0.0 reduce-scatter.2.cloned.1.call-update
  151.4 36.6 %all_to_all.21 = bf16[256,8,128]{2,1,0:T(8,128)(2,1)S(1)} all-to-all(bf16[256,8,128]{2,1,0:T(8,128)(2,1)S(1)} %bitcast.48), channel_id=1, replica_groups=mesh['dp'=32,'head'=8] {'dp','head'}, dimensions={0} | all-to-all | bytes 1048576 | tf_op jit(solution)/shard_map/all_to_all | solution.py:128
  188.0 0.2 reshape.76
  188.2 0.3 reduce_sum.12
  188.6 0.3 fusion.1
  188.9 0.9 broadcast_in_dim.39
  189.7 5.8 %all-to-all-start.3 = ((bf16[256,8,128]{2,1,0:T(8,128)(2,1)}), bf16[256,8,128]{2,1,0:T(8,128)(2,1)S(1)}, u32[]{:S(2)}, u32[]{:S(2)}) async-start(bf16[256,8,128]{2,1,0:T(8,128)(2,1)} %bitcast.16), calls=%async_computation.4 | async-start | bytes 1048576 | tf_op jit(solution)/shard_map/all_to_all | solution.py:128
  195.6 26.9 %all-to-all-done.3 = bf16[256,8,128]{2,1,0:T(8,128)(2,1)S(1)} async-done(((bf16[256,8,128]{2,1,0:T(8,128)(2,1)}), bf16[256,8,128]{2,1,0:T(8,128)(2,1)S(1)}, u32[]{:S(2)}, u32[]{:S(2)}) %all-to-all-start.3) | async-done | bytes 524320 | tf_op jit(solution)/shard_map/all_to_all | solution.py:128
  222.5 0.1 convert_select_fusion
  222.6 5.4 %reduce-scatter.2.cloned.1.call-done = bf16[1,2,128,1024]{3,2,1,0:T(8,128)(2,1)} async-done(((bf16[8,2,128,1024]{3,2,1,0:T(8,128)(2,1)}), bf16[1,2,128,1024]{3,2,1,0:T(8,128)(2,1)}) %reduce-scatter.2.cloned.1.call-update) | async-done | bytes 524304 | tf_op jit(solution)/shard_map/reduce_scatter | solution.py:153
  228.0 1.2 fusion.2
  229.2 0.8 slice_bitcast_fusion
  (4 shorter events, 0.0 us)
Async XLA Ops:
  7.2 84.5 %all-gather.3.cloned.1.call-start = ((), (), s32[]{:S(2)}) async-start(), calls=%async_computation.6 | async-start | bytes 4718592 | tf_op jit(solution)/shard_map/all_gather | solution.py:135
  9.1 43.4 %copy-start.3 = (s32[32]{0:T(128)S(1)}, s32[32]{0:T(128)}, u32[]{:S(2)}) copy-start(s32[32]{0:T(128)} %param.12) | copy-start | bytes 388
  10.2 49.3 %copy-start.4 = (s32[32]{0:T(128)S(1)}, s32[32]{0:T(128)}, u32[]{:S(2)}) copy-start(s32[32]{0:T(128)} %param.13) | copy-start | bytes 388
  10.2 50.6 %copy-start.2 = (s32[1024]{0:T(1024)S(1)}, s32[1024]{0:T(1024)}, u32[]{:S(2)}) copy-start(s32[1024]{0:T(1024)} %param.11) | copy-start | bytes 12292
  53.6 32.7 %all-to-all-start.1 = ((bf16[256,8,128]{2,1,0:T(8,128)(2,1)}), bf16[256,8,128]{2,1,0:T(8,128)(2,1)S(1)}, u32[]{:S(2)}, u32[]{:S(2)}) async-start(bf16[256,8,128]{2,1,0:T(8,128)(2,1)} %bitcast.8), calls=%async_computation.1 | async-start | bytes 1048576 | tf_op jit(solution)/shard_map/all_to_all | solution.py:128
  59.5 168.5 %reduce-scatter.2.cloned.1.call-start = ((), (), s32[]{:S(2)}) async-start(), calls=%async_computation.5 | async-start | bytes 4718592 | tf_op jit(solution)/shard_map/reduce_scatter | solution.py:153
  91.6 1.6 copy-start
  93.2 1.6 copy-start.1
  189.7 32.8 %all-to-all-start.3 = ((bf16[256,8,128]{2,1,0:T(8,128)(2,1)}), bf16[256,8,128]{2,1,0:T(8,128)(2,1)S(1)}, u32[]{:S(2)}, u32[]{:S(2)}) async-start(bf16[256,8,128]{2,1,0:T(8,128)(2,1)} %bitcast.16), calls=%async_computation.4 | async-start | bytes 1048576 | tf_op jit(solution)/shard_map/all_to_all | solution.py:128
Sparse Core Ops, SparseCore 0:
  10.4 81.2 all-gather.2
  151.5 76.4 reduce-scatter.1
where the time goes:
time: 237 us
  blocking collectives  78.5 us (33%)
  waiting for transfers between devices  62.8 us (26%)
  Pallas kernels  56.6 us (24%)
  between operations  14.8 us (6%)
  starting transfers between devices  11.8 us (5%)
  local copies, waits for them, and re-layouts  6.96 us (3%)
  other arithmetic  4.98 us (2%)
    all_to_all x2, blocking collectives, exchange(): lax.all_to_all(pieces, ('dp', 'head'), split_axis=0, concat_axis=0, tiled...  78.5 us
    pallas_call x1, Pallas kernels, attend(): pl.pallas_call(body, grid=(KV_HEADS,), in_specs=[pl.BlockSpec((KEYS, ROWS...  56.6 us
    all_to_all x2, waiting for transfers between devices, exchange(): lax.all_to_all(pieces, ('dp', 'head'), split_axis=0, concat_axis=0, tiled...  52 us
    all_to_all x2, starting transfers between devices, exchange(): lax.all_to_all(pieces, ('dp', 'head'), split_axis=0, concat_axis=0, tiled...  11.7 us
    reduce_scatter x1, waiting for transfers between devices, per_device(): home = lax.psum_scatter(dnear, 'head', scatter_dimension=0)  5.44 us
    all_gather x1, waiting for transfers between devices, per_device(): near = lax.all_gather(kv, 'head', axis=0)  5.31 us
  transfers between devices with their start and end apart: 4, of which 4 were waited for; matrix products, arithmetic and copies ran while one was open for 2% of the time, Pallas kernels for 0%

commit v1 on v0

v1 whole, which is shorter than its diff:
```python
import functools

import jax
import jax.numpy as jnp
from jax import lax
from jax.experimental import pallas as pl
from jax.experimental.pallas import tpu as pltpu
from jax.sharding import PartitionSpec as P

HEAD = 128
GROUP = 8
KV_HEADS = 8
ROWS = 128
WIDE = GROUP * ROWS
TAIL = 128
PAIR = 256
LOG2E = 1.4426950408889634
SCALE = HEAD**-0.5
MASKED = -1e30
F32 = jnp.float32
BF16 = jnp.bfloat16
NT = (((1,), (1,)), ((), ()))
TN = (((0,), (0,)), ((), ()))
BLOCK = 512
VMEM = 60 * 2**20


def dot(a, b, dims=(((1,), (0,)), ((), ()))):
    return lax.dot_general(a, b, dims, preferred_element_type=F32)


def fold(x, op):
    return op(x.reshape(x.shape[0] // 8, 8, x.shape[1]), axis=0)


def heads(ref):
    return jnp.concatenate([ref[:, g * HEAD : (g + 1) * HEAD] for g in range(GROUP)], axis=0)


SLICES = [slice(at, at + PAIR) for at in range(0, WIDE, PAIR)]


def stagger(*stages):
    for step in range(len(SLICES) + len(stages) - 1):
        for late, stage in enumerate(stages):
            if 0 <= step - late < len(SLICES):
                stage(SLICES[step - late])


def score(keys, q2, mask):
    return dot(keys, q2, NT) * (SCALE * LOG2E) + jnp.concatenate([mask, mask], axis=1)


def absorb(keys, values, mask, qs, stat, acc, s_ref, p_ref):
    size = keys.shape[0]
    kept = {}

    def scores(at):
        s = score(keys, qs[at], mask)
        s_ref[:size, at] = s
        top = jnp.max(fold(s, jnp.max), axis=0, keepdims=True)
        kept[at.start] = jnp.maximum(stat[0, 0:1, at], top)

    def weights(at):
        high = kept[at.start]
        p = jnp.exp2(s_ref[:size, at] - high)
        p_ref[:size, at] = p.astype(BF16)
        alpha = jnp.exp2(stat[0, 0:1, at] - high)
        stat[0, 0:1, at] = high
        stat[0, 1:2, at] = stat[0, 1:2, at] * alpha + jnp.sum(fold(p, jnp.sum), axis=0, keepdims=True)
        kept[at.start] = alpha

    def mix(at):
        acc[0, :, at] = acc[0, :, at] * kept[at.start] + dot(values, p_ref[:size, at], TN)

    stagger(scores, weights, mix)


def spread(keys, values, mask, qs, dos, stat, dq, s_ref, d_ref, p_ref, ds_ref):
    size = keys.shape[0]
    sums = [0.0, 0.0]

    def scores(at):
        s_ref[:size, at] = score(keys, qs[at], mask) - stat[0, 0:1, at]
        d_ref[:size, at] = dot(values, dos[at], NT) - stat[0, 1:2, at]

    def weights(at):
        p = jnp.exp2(s_ref[:size, at])
        p_ref[:size, at] = p.astype(BF16)
        ds_ref[:size, at] = (p * d_ref[:size, at]).astype(BF16)

    def mix(at):
        sums[0] = sums[0] + dot(ds_ref[:size, at], qs[at])
        sums[1] = sums[1] + dot(p_ref[:size, at], dos[at])
        dq[0, :, at] += dot(keys, ds_ref[:size, at], TN)

    stagger(scores, weights, mix)
    return (sums[0] * SCALE).astype(BF16), sums[1].astype(BF16)


def blocks(span, near, bias, work):
    @pl.loop(span[0], span[1])
    def _(j):
        part = pl.ds(BLOCK // ROWS * j, BLOCK // ROWS)
        keys = near[part, 0].reshape(BLOCK, HEAD)
        values = near[part, 1].reshape(BLOCK, HEAD)
        work(part, keys, values, bias[pl.ds(pl.multiple_of(j * BLOCK, BLOCK), BLOCK)])


def near_fwd_body(span, bias, q_ref, near, stat, acc, qs, s_ref, p_ref):
    qs[...] = heads(q_ref)
    stat[0, 0:1] = jnp.full((1, WIDE), MASKED, F32)
    stat[0, 1:2] = jnp.zeros((1, WIDE), F32)
    acc[...] = jnp.zeros_like(acc)

    def work(part, keys, values, mask):
        absorb(keys, values, mask, qs, stat, acc, s_ref, p_ref)

    blocks(span, near, bias, work)


def tail(far):
    return far[:, 0].reshape(TAIL, HEAD), far[:, 1].reshape(TAIL, HEAD)


def far_body(
    flag, bias, q_ref, do_ref, far, stat_in, acc_in, o_ref, stat_out, dq, dfar, qs, dos, stat, acc, s_ref, d_ref, p_ref, ds_ref
):
    stat[...] = stat_in[...]
    acc[...] = acc_in[...]
    dq[...] = jnp.zeros_like(dq)

    @pl.when(flag[0] > 0)
    def _():
        qs[...] = heads(q_ref)
        dos[...] = heads(do_ref)
        absorb(*tail(far), bias[...], qs, stat, acc, s_ref, p_ref)

    norm = stat[0, 1:2]
    out = (acc[0] * (1.0 / norm)).astype(BF16)
    stat_out[0, 0:1] = stat[0, 0:1] + jnp.log2(norm)
    for g in range(GROUP):
        at = slice(g * HEAD, (g + 1) * HEAD)
        o_ref[:, at] = out[:, at].T
        prod = do_ref[:, at].T.astype(F32) * out[:, at].astype(F32)
        stat_out[0, 1:2, at] = jnp.sum(prod, axis=0, keepdims=True)

    @pl.when(flag[0] > 0)
    def _():
        dk, dv = spread(*tail(far), bias[...], qs, dos, stat_out, dq, s_ref, d_ref, p_ref, ds_ref)
        dfar[:, 0] = dk.reshape(8, 16, HEAD)
        dfar[:, 1] = dv.reshape(8, 16, HEAD)

    @pl.when(flag[0] == 0)
    def _():
        dfar[...] = jnp.zeros_like(dfar)


def near_bwd_body(span, bias, q_ref, do_ref, near, stat, dq_in, *refs):
    dq_ref, dnear, qs, dos, dq, s_ref, d_ref, p_ref, ds_ref = refs[-9:]
    qs[...] = heads(q_ref)
    dos[...] = heads(do_ref)
    dq[...] = dq_in[...]
    dnear[...] = jnp.zeros_like(dnear)

    def work(part, keys, values, mask):
        dk, dv = spread(keys, values, mask, qs, dos, stat, dq, s_ref, d_ref, p_ref, ds_ref)
        dnear[part, 0] = dk.reshape(BLOCK // ROWS, ROWS, HEAD)
        dnear[part, 1] = dv.reshape(BLOCK // ROWS, ROWS, HEAD)

    blocks(span, near, bias, work)
    for g in range(GROUP):
        at = slice(g * HEAD, (g + 1) * HEAD)
        dq_ref[:, at] = (dq[0, :, at] * SCALE).astype(BF16).T


def shape(dims, dtype=BF16):
    return jax.ShapeDtypeStruct(dims, dtype)


STAT = shape((KV_HEADS, 2, WIDE), F32)
ACC = shape((KV_HEADS, HEAD, WIDE), F32)
TALL = shape((WIDE, HEAD))


def spec(a, skip=0):
    if len(a.shape) == 2:
        return pl.BlockSpec((ROWS, WIDE), lambda k: (0, k + skip))
    if len(a.shape) == 4:
        return pl.BlockSpec(a.shape[:3] + (HEAD,), lambda k: (0, 0, 0, k + skip))
    return pl.BlockSpec((1,) + a.shape[1:], lambda k: (k + skip, 0, 0))


def call(body, scalars, bias, args, outs, scratch, keys, products, skip=0, count=KV_HEADS, onto=()):
    size = keys * WIDE * count
    return pl.pallas_call(
        body,
        grid=(count,),
        in_specs=[pl.BlockSpec(memory_space=pltpu.SMEM), pl.BlockSpec(bias.shape, lambda k: (0, 0))]
        + [spec(a, skip) for a in args]
        + [pl.BlockSpec(memory_space=pl.ANY) for a in onto],
        out_specs=[spec(a, skip) for a in outs],
        out_shape=outs,
        scratch_shapes=[pltpu.VMEM(a.shape, a.dtype) for a in scratch],
        input_output_aliases={2 + len(args) + i: i for i in range(len(onto))},
        compiler_params=pltpu.CompilerParams(vmem_limit_bytes=VMEM),
        cost_estimate=pl.CostEstimate(
            flops=4 * products * HEAD * size, bytes_accessed=16 * 2**20, transcendentals=size
        ),
    )(scalars, bias, *args, *onto)


ONE_STAT = shape((1, 2, WIDE), F32)
ONE_ACC = shape((1, HEAD, WIDE), F32)


def slabs(keys):
    return [shape((keys, WIDE), F32), shape((keys, WIDE), F32), shape((keys, WIDE)), shape((keys, WIDE))]


def near_fwd(span, bias, q, near):
    scratch = [TALL, shape((BLOCK, WIDE), F32), shape((BLOCK, WIDE))]
    return call(near_fwd_body, span, bias, [q, near], [STAT, ACC], scratch, 1024, 2)


def far_both(flag, bias, q, grad, far, stat, acc):
    outs = [shape(q.shape), STAT, ACC, shape(far.shape)]
    scratch = [TALL, TALL, ONE_STAT, ONE_ACC, *slabs(TAIL)]
    return call(far_body, flag, bias, [q, grad, far, stat, acc], outs, scratch, TAIL, 12)


def near_bwd(span, bias, q, grad, near, stat, dq, skip, onto=()):
    outs = [shape(q.shape), shape(near.shape)]
    scratch = [TALL, TALL, ONE_ACC, *slabs(BLOCK)]
    args = [q, grad, near, stat, dq]
    return call(near_bwd_body, span, bias, args, outs, scratch, 1024, 5, skip, KV_HEADS // 2, onto)


def split(block):
    rows = block.shape[1] // 8
    return block.reshape(2, rows, 8, 8, HEAD).transpose(0, 1, 3, 2, 4).reshape(16 * rows, 8, HEAD)


def join(pieces):
    rows = pieces.shape[0] // 16
    return pieces.reshape(2, rows, 8, 8, HEAD).transpose(0, 1, 3, 2, 4).reshape(2, rows * 8, 1024)


def swap(pieces, axis):
    return lax.all_to_all(pieces, axis, split_axis=0, concat_axis=0, tiled=True)


def route(block, choose):
    pieces = swap(split(block), "dp").reshape(32, 8 * HEAD)
    pieces = jnp.dot(choose, pieces, preferred_element_type=F32).astype(BF16)
    return join(swap(pieces.reshape(32, 8, HEAD), "dp"))


def scatter_last(kv, z):
    half = lax.ppermute(kv[:, :64], "head", [(7, 3)])
    mine = jnp.where(z == 7, kv[:, 64:], half)
    send = jnp.where(z == 7, mine[:, :32], half[:, :32])
    quarter = lax.ppermute(send, "head", [(7, 5), (3, 1)])
    send = jnp.where(z % 4 == 3, mine[:, 32:48], quarter[:, :16])
    eighth = lax.ppermute(send, "head", [(7, 6), (5, 4), (3, 2), (1, 0)])
    return jnp.where(z % 2 == 0, eighth, jnp.where(z % 4 == 1, quarter[:, 16:], mine[:, 48:]))


def collect_last(piece):
    two = lax.ppermute(piece, "head", [(i, i + 1) for i in (0, 2, 4, 6)])
    two = jnp.concatenate([two, piece], axis=1)
    four = lax.ppermute(two, "head", [(1, 3), (5, 7)])
    four = jnp.concatenate([four, two], axis=1)
    eight = lax.ppermute(four, "head", [(3, 7)])
    return jnp.concatenate([eight, four], axis=1)


def per_device(queries, input_keys, input_values, output_gradient, doc_ids, spill_src, spill_len):
    rank, z = lax.axis_index("dp"), lax.axis_index("head")
    ids = jnp.arange(32, dtype=jnp.int32)
    kv = jnp.stack([input_keys, input_values])
    near = lax.all_gather(kv, "head", axis=0)

    wanted = (spill_src[:, None] == ids[None, :]).astype(BF16)
    piece = route(scatter_last(kv, z), wanted)
    near, piece = lax.optimization_barrier((near, piece))
    far = swap(jnp.broadcast_to(piece[None], (8, 2, 16, 1024)), "head")

    place = jnp.arange(1024, dtype=jnp.int32)
    row_at = z * ROWS + jnp.arange(ROWS, dtype=jnp.int32)
    row_docs = lax.dynamic_slice_in_dim(doc_ids, z * ROWS, ROWS)
    near_seen = (doc_ids[:, None] == row_docs[None, :]) & (place[:, None] <= row_at[None, :])
    far_seen = (place[:TAIL, None] >= TAIL - spill_len[rank]) & (row_docs[None, :] == 0)
    near_bias = jnp.where(near_seen, 0.0, MASKED).astype(F32)
    far_bias = jnp.where(far_seen, 0.0, MASKED).astype(F32)
    closing = doc_ids.reshape(8, ROWS)[:, ROWS - 1]
    begin = jnp.sum((closing < row_docs[0]).astype(jnp.int32))
    span = jnp.stack([begin // 4, z // 4 + 1])
    flag = (row_docs[:1] == 0).astype(jnp.int32)

    stat, acc = near_fwd(span, near_bias, queries, near)
    out, stat, dq, dfar = far_both(flag, far_bias, queries, output_gradient, far, stat, acc)
    parts = swap(dfar, "head")
    args = (span, near_bias, queries, output_gradient, near, stat, dq)
    half = near_bwd(*args, 0)
    half, parts = lax.optimization_barrier((half, parts))
    dq, dnear = near_bwd(*args, KV_HEADS // 2, half)

    home = lax.psum_scatter(dnear, "head", scatter_dimension=0)
    piece = jnp.sum(parts.astype(F32), axis=0).astype(BF16)
    returned = collect_last(route(piece, wanted.T))
    returned = jnp.where(z == 7, returned.astype(F32), 0.0)
    total = (home.astype(F32) + returned).astype(BF16)
    return out, dq, total[0], total[1]


def solution(mesh):
    rows = P(("dp", "head"), None)
    return jax.shard_map(
        per_device,
        mesh=mesh,
        in_specs=(rows, rows, rows, rows, P("dp"), P(), P()),
        out_specs=(rows, rows, rows, rows),
        check_vma=False,
    )
```

time: 237 us -> 218 us (0.920); the launches traced: 237 us -> 214 us
  blocking collectives: 78.5 us -> 28.3 us
  waiting for transfers between devices: 62.8 us -> 80.3 us
  starting transfers between devices: 11.8 us -> 28.2 us
  Pallas kernels: 56.6 us -> 44.8 us
  other arithmetic: 4.98 us -> 10.5 us
  between operations: 14.8 us -> 17.6 us
  local copies, waits for them, and re-layouts: 6.96 us -> 4.39 us
    all_to_all x2, blocking collectives: 78.5 us -> 28.3 us  [swap(): return lax.all_to_all(pieces, axis, split_axis=0, concat_axis=0, tiled=True)]
    all_to_all x2 -> x4, waiting for transfers between devices: 52 us -> 23 us  [swap(): return lax.all_to_all(pieces, axis, split_axis=0, concat_axis=0, tiled=True)]
    reduce_scatter x1, waiting for transfers between devices: 5.44 us -> 31.8 us  [per_device(): home = lax.psum_scatter(dnear, 'head', scatter_dimension=0)]
    ppermute x0 -> x6, waiting for transfers between devices: none -> 25.4 us  [the longest x1 22.6 us: scatter_last(): eighth = lax.ppermute(send, 'head', [(7, 6), (5, 4), (3, 2), (1, 0)])]
    pallas_call x1 -> x4, Pallas kernels: 56.6 us -> 44.8 us  [call(): pl.pallas_call(body, grid=(count,), in_specs=[pl.BlockSpec(memory_space=p...]
    all_to_all x2 -> x4, starting transfers between devices: 11.7 us -> 21.9 us  [swap(): return lax.all_to_all(pieces, axis, split_axis=0, concat_axis=0, tiled=True)]
    ppermute x0 -> x6, starting transfers between devices: none -> 6.17 us  [the longest x1 2.18 us: collect_last(): two = lax.ppermute(piece, 'head', [(i, i + 1) for i in (0, 2, 4, 6)])]
    all_gather x1, waiting for transfers between devices: 5.31 us -> 0.01 us  [per_device(): near = lax.all_gather(kv, 'head', axis=0)]
  transfers between devices with their start and end apart: 4 -> 12, of which waited for: 4 -> 7; matrix products, arithmetic and copies ran while one was open for 2% -> 5% of each run, Pallas kernels for 0% -> 10%
where the time goes in v1:
time: 218 us; the launch traced here: 214 us
  waiting for transfers between devices  80.3 us (37%)
  Pallas kernels  44.8 us (21%)
  blocking collectives  28.3 us (13%)
  starting transfers between devices  28.2 us (13%)
  between operations  17.6 us (8%)
  other arithmetic  10.5 us (5%)
  local copies, waits for them, and re-layouts  4.39 us (2%)
    pallas_call x4, Pallas kernels, call(): pl.pallas_call(body, grid=(count,), in_specs=[pl.BlockSpec(memory_space=p...  44.8 us
    reduce_scatter x1, waiting for transfers between devices, per_device(): home = lax.psum_scatter(dnear, 'head', scatter_dimension=0)  31.8 us
    all_to_all x2, blocking collectives, swap(): return lax.all_to_all(pieces, axis, split_axis=0, concat_axis=0, tiled=True)  28.3 us
    all_to_all x4, waiting for transfers between devices, swap(): return lax.all_to_all(pieces, axis, split_axis=0, concat_axis=0, tiled=True)  23 us
    ppermute x1, waiting for transfers between devices, scatter_last(): eighth = lax.ppermute(send, 'head', [(7, 6), (5, 4), (3, 2), (1, 0)])  22.6 us
    all_to_all x4, starting transfers between devices, swap(): return lax.all_to_all(pieces, axis, split_axis=0, concat_axis=0, tiled=True)  21.9 us
  transfers between devices with their start and end apart: 12, of which 7 were waited for; matrix products, arithmetic and copies ran while one was open for 5% of the time, Pallas kernels for 10%

profile of v1, /device:TPU:1, one launch (start us, length us, event | category | flops | bytes accessed | tf_op | source)
XLA Modules:
  0.0 214.5 jit_solution(14914678434340107428)
XLA Ops:
  7.2 0.0 copy-start.1
  7.2 0.0 copy-start.2
  7.2 0.0 all-gather.3.cloned.1.call-start
  7.2 1.9 pad_maximum_fusion
  9.1 0.0 all-gather.3.cloned.1.call-update
  9.1 1.0 fusion.7
  10.1 0.7 collective-permute-start
  10.8 1.2 dynamic_slice.7
  12.7 0.8 broadcast_compare_fusion
  13.5 0.0 collective-permute-done
  13.5 1.0 fusion.6
  14.5 0.7 collective-permute-start.1
  15.2 1.7 fusion.4.bias
  17.0 0.0 collective-permute-done.1
  17.0 1.3 collective-permute-start.2
  18.3 22.6 %collective-permute-done.2 = bf16[2,16,1024]{2,1,0:T(8,128)(2,1)S(1)} collective-permute-done((bf16[2,16,1024]{2,1,0:T(8,128)(2,1)S(1)}, bf16[2,16,1024]{2,1,0:T(8,128)(2,1)S(1)}, u32[]{:S(2)}, u32[]{:S(2)}) %collective-permute-start.2) | collective-permute-done | bytes 65568 | tf_op jit(solution)/shard_map/ppermute | solution.py:265
  40.9 0.6 fusion.12
  41.6 10.3 %all-to-all-start = ((bf16[32,8,128]{2,1,0:T(8,128)(2,1)}), bf16[32,8,128]{2,1,0:T(8,128)(2,1)S(1)}, u32[]{:S(2)}, u32[]{:S(2)}) async-start(bf16[32,8,128]{2,1,0:T(8,128)(2,1)} %bitcast.6), calls=%async_computation | async-start | bytes 131072 | tf_op jit(solution)/shard_map/all_to_all | solution.py:250
  51.9 0.7 and_select_fusion.bias
  52.6 6.6 %all-to-all-done = bf16[32,8,128]{2,1,0:T(8,128)(2,1)S(1)} async-done(((bf16[32,8,128]{2,1,0:T(8,128)(2,1)}), bf16[32,8,128]{2,1,0:T(8,128)(2,1)S(1)}, u32[]{:S(2)}, u32[]{:S(2)}) %all-to-all-start) | async-done | bytes 65568 | tf_op jit(solution)/shard_map/all_to_all | solution.py:250
  59.2 0.0 copy-done.2
  59.2 0.2 fusion
  59.4 0.7 copy.16
  60.1 3.9 %all-to-all-start.1 = ((bf16[32,8,128]{2,1,0:T(8,128)(2,1)}), bf16[32,8,128]{2,1,0:T(8,128)(2,1)S(1)}, u32[]{:S(2)}, u32[]{:S(2)}) async-start(bf16[32,8,128]{2,1,0:T(8,128)(2,1)} %bitcast.35), calls=%async_computation.1 | async-start | bytes 131072 | tf_op jit(solution)/shard_map/all_to_all | solution.py:250
  64.0 0.0 copy-done.1
  64.0 0.7 convert_reduce_fusion
  67.4 4.0 %all-to-all-done.1 = bf16[32,8,128]{2,1,0:T(8,128)(2,1)S(1)} async-done(((bf16[32,8,128]{2,1,0:T(8,128)(2,1)}), bf16[32,8,128]{2,1,0:T(8,128)(2,1)S(1)}, u32[]{:S(2)}, u32[]{:S(2)}) %all-to-all-start.1) | async-done | bytes 65568 | tf_op jit(solution)/shard_map/all_to_all | solution.py:250
  71.4 0.0 all-gather.3.cloned.1.call-done
  71.4 0.9 broadcast_in_dim.36
  72.3 3.6 %all-to-all-start.2 = ((bf16[8,2,16,1024]{3,2,1,0:T(8,128)(2,1)}), bf16[8,2,16,1024]{3,2,1,0:T(8,128)(2,1)S(1)}, u32[]{:S(2)}, u32[]{:S(2)}) async-start(bf16[8,2,16,1024]{3,2,1,0:T(8,128)(2,1)} %broadcast_in_dim.36), calls=%async_computation.2 | async-start | bytes 1048576 | tf_op jit(solution)/shard_map/all_to_all | solution.py:250
  75.9 0.7 pad_add_fusion.span
  76.5 11.8 %shard_map.102 = (f32[8,2,1024]{2,1,0:T(2,128)}, f32[8,128,1024]{2,1,0:T(8,128)}) custom-call(s32[2]{0:T(128)} %pad_add_fusion.span, f32[1024,128]{1,0:T(8,128)} %fusion.4.bias, bf16[128,8192]{1,0:T(8,128)(2,1)} %q_ref.7, bf16[8,2,128,1024]{3,2,1,0:T(8,128)(2,1)} %bitcast.68), custom_call_target="tpu_custom_call" | custom-call | flops 8589934592 | bytes 16777216 | tf_op jit(solution)/shard_map/pallas_call | solution.py:196
  88.3 5.5 %all-to-all-done.2.far = bf16[8,2,16,1024]{3,2,1,0:T(8,128)(2,1)S(1)} async-done(((bf16[8,2,16,1024]{3,2,1,0:T(8,128)(2,1)}), bf16[8,2,16,1024]{3,2,1,0:T(8,128)(2,1)S(1)}, u32[]{:S(2)}, u32[]{:S(2)}) %all-to-all-start.2) | async-done | bytes 524320 | tf_op jit(solution)/shard_map/all_to_all | solution.py:250
  93.8 0.0 copy-start
  93.8 0.8 copy-done
  94.6 14.1 %shard_map.103 = (bf16[128,8192]{1,0:T(8,128)(2,1)}, f32[8,2,1024]{2,1,0:T(2,128)}, f32[8,128,1024]{2,1,0:T(8,128)}, bf16[8,2,16,1024]{3,2,1,0:T(8,128)(2,1)}) custom-call(s32[1]{0:T(128)S(6)} %convert_element_type.28.flag, f32[128,128]{1,0:T(8,128)} %and_select_fusion.bias, bf16[128,8192]{1,0:T(8,128)(2,1)} %q_ref.7, bf16[128,8192]{1,0:T(8,128)(2,1)} %do_ref.5, ...), custom_call_target="tpu_custom_call" | custom-call | flops 6442450944 | bytes 16777216 | tf_op jit(solution)/shard_map/pallas_call | solution.py:196
  108.7 4.1 %all-to-all-start.3 = ((bf16[8,2,16,1024]{3,2,1,0:T(8,128)(2,1)}), bf16[8,2,16,1024]{3,2,1,0:T(8,128)(2,1)S(1)}, u32[]{:S(2)}, u32[]{:S(2)}) async-start(bf16[8,2,16,1024]{3,2,1,0:T(8,128)(2,1)} %get-tuple-element.28), calls=%async_computation.3 | async-start | bytes 1048576 | tf_op jit(solution)/shard_map/all_to_all | solution.py:250
  112.8 0.0 reduce-scatter.2.cloned.1.call-start
  112.9 9.4 %shard_map.104 = (bf16[128,8192]{1,0:T(8,128)(2,1)}, bf16[8,2,128,1024]{3,2,1,0:T(8,128)(2,1)}) custom-call(s32[2]{0:T(128)} %pad_add_fusion.span, f32[1024,128]{1,0:T(8,128)} %fusion.4.bias, bf16[128,8192]{1,0:T(8,128)(2,1)} %q_ref.7, bf16[128,8192]{1,0:T(8,128)(2,1)} %do_ref.5, bf16[8,2,128,1024]{3,2,1,0:T(8,128)(2,1)} %bitcast.69, ...), custom_call_target="tpu_custom_call" | custom-call | flops 10737418240 | bytes 16777216 | tf_op jit(solution)/shard_map/pallas_call | solution.py:196
  122.3 6.9 %all-to-all-done.3 = bf16[8,2,16,1024]{3,2,1,0:T(8,128)(2,1)S(1)} async-done(((bf16[8,2,16,1024]{3,2,1,0:T(8,128)(2,1)}), bf16[8,2,16,1024]{3,2,1,0:T(8,128)(2,1)S(1)}, u32[]{:S(2)}, u32[]{:S(2)}) %all-to-all-start.3) | async-done | bytes 524320 | tf_op jit(solution)/shard_map/all_to_all | solution.py:250
  129.2 9.4 %shard_map.105 = (bf16[128,8192]{1,0:T(8,128)(2,1)}, bf16[8,2,128,1024]{3,2,1,0:T(8,128)(2,1)}) custom-call(s32[2]{0:T(128)} %pad_add_fusion.span, f32[1024,128]{1,0:T(8,128)} %fusion.4.bias, bf16[128,8192]{1,0:T(8,128)(2,1)} %q_ref.7, bf16[128,8192]{1,0:T(8,128)(2,1)} %do_ref.5, ...), custom_call_target="tpu_custom_call", output_to_operand_aliasing={{0}: (7, {}), {1}: (8, {})} | custom-call | flops 10737418240 | bytes 16777216 | tf_op jit(solution)/shard_map/pallas_call | solution.py:196
  138.7 0.0 reduce-scatter.2.cloned.1.call-update
  138.7 0.1 reduce_sum.22
  138.8 17.4 %all_to_all.30 = bf16[32,8,128]{2,1,0:T(8,128)(2,1)S(1)} all-to-all(bf16[32,8,128]{2,1,0:T(8,128)(2,1)S(1)} %bitcast.64), channel_id=1, replica_groups=mesh['dp'=32,'head'=8] {'dp'}, dimensions={0} | all-to-all | bytes 131072 | tf_op jit(solution)/shard_map/all_to_all | solution.py:250
  156.2 0.3 fusion.1
  156.5 10.9 %all_to_all.31 = bf16[32,8,128]{2,1,0:T(8,128)(2,1)S(1)} all-to-all(bf16[32,8,128]{2,1,0:T(8,128)(2,1)S(1)} %bitcast.63), channel_id=1, replica_groups=mesh['dp'=32,'head'=8] {'dp'}, dimensions={0} | all-to-all | bytes 131072 | tf_op jit(solution)/shard_map/all_to_all | solution.py:250
  167.4 2.2 %collective-permute-start.3 = (bf16[2,16,1024]{2,1,0:T(8,128)(2,1)S(1)}, bf16[2,16,1024]{2,1,0:T(8,128)(2,1)S(1)}, u32[]{:S(2)}, u32[]{:S(2)}) collective-permute-start(bf16[2,16,1024]{2,1,0:T(8,128)(2,1)S(1)} %bitcast.56), channel_id=1, source_target_pairs={{0,1},{2,3},{4,5},{6,7},{8,9},{10,11},{12,13},{14,15},{16,17},{18,... | collective-permute-start | bytes 196616 | tf_op jit(solution)/shard_map/ppermute | solution.py:270
  169.6 2.8 %collective-permute-done.3 = bf16[2,16,1024]{2,1,0:T(8,128)(2,1)S(1)} collective-permute-done((bf16[2,16,1024]{2,1,0:T(8,128)(2,1)S(1)}, bf16[2,16,1024]{2,1,0:T(8,128)(2,1)S(1)}, u32[]{:S(2)}, u32[]{:S(2)}) %collective-permute-start.3) | collective-permute-done | bytes 65568 | tf_op jit(solution)/shard_map/ppermute | solution.py:270
  172.3 0.7 collective-permute-start.4
  173.0 0.0 collective-permute-done.4
  173.1 0.7 collective-permute-start.5
  173.7 0.0 collective-permute-done.5
  173.7 31.8 %reduce-scatter.2.cloned.1.call-done = bf16[1,2,128,1024]{3,2,1,0:T(8,128)(2,1)} async-done(((bf16[8,2,128,1024]{3,2,1,0:T(8,128)(2,1)}), bf16[1,2,128,1024]{3,2,1,0:T(8,128)(2,1)}) %reduce-scatter.2.cloned.1.call-update) | async-done | bytes 524304 | tf_op jit(solution)/shard_map/reduce_scatter | solution.py:309
  205.6 1.2 fusion.2
  206.8 0.8 slice_bitcast_fusion
  (8 shorter events, 0.1 us)
Async XLA Ops:
  7.2 56.9 %copy-start.1 = (s32[1024]{0:T(1024)S(1)}, s32[1024]{0:T(1024)}, u32[]{:S(2)}) copy-start(s32[1024]{0:T(1024)} %param.11) | copy-start | bytes 12292
  7.2 52.1 %copy-start.2 = (s32[32]{0:T(128)S(1)}, s32[32]{0:T(128)}, u32[]{:S(2)}) copy-start(s32[32]{0:T(128)} %param.12) | copy-start | bytes 388
  7.2 64.3 %all-gather.3.cloned.1.call-start = ((), (), s32[]{:S(2)}) async-start(), calls=%async_computation.8 | async-start | bytes 4718592 | tf_op jit(solution)/shard_map/all_gather | solution.py:282
  10.1 3.4 %collective-permute-start = (bf16[2,64,1024]{2,1,0:T(8,128)(2,1)S(1)}, bf16[2,64,1024]{2,1,0:T(8,128)(2,1)S(1)}, u32[]{:S(2)}, u32[]{:S(2)}) collective-permute-start(bf16[2,64,1024]{2,1,0:T(8,128)(2,1)S(1)} %fusion.7), channel_id=1, source_target_pairs={{7,3},{15,11},{23,19},{31,27},{39,35},{47,43},{55,51},{63,59},{71,... | collective-permute-start | bytes 786440 | tf_op jit(solution)/shard_map/ppermute | solution.py:260
  14.5 2.4 %collective-permute-start.1 = (bf16[2,32,1024]{2,1,0:T(8,128)(2,1)S(1)}, bf16[2,32,1024]{2,1,0:T(8,128)(2,1)S(1)}, u32[]{:S(2)}, u32[]{:S(2)}) collective-permute-start(bf16[2,32,1024]{2,1,0:T(8,128)(2,1)S(1)} %slice_select_fusion), channel_id=1, source_target_pairs={{7,5},{3,1},{15,13},{11,9},{23,21},{19,17},{31,29},{27,25},{39,37}... | collective-permute-start | bytes 393224 | tf_op jit(solution)/shard_map/ppermute | solution.py:263
  17.0 24.0 %collective-permute-start.2 = (bf16[2,16,1024]{2,1,0:T(8,128)(2,1)S(1)}, bf16[2,16,1024]{2,1,0:T(8,128)(2,1)S(1)}, u32[]{:S(2)}, u32[]{:S(2)}) collective-permute-start(bf16[2,16,1024]{2,1,0:T(8,128)(2,1)S(1)} %slice_select_fusion.2), channel_id=1, source_target_pairs={{7,6},{5,4},{3,2},{1,0},{15,14},{13,12},{11,10},{9,8},{23,22},{21,... | collective-permute-start | bytes 196616 | tf_op jit(solution)/shard_map/ppermute | solution.py:265
  41.6 17.7 %all-to-all-start = ((bf16[32,8,128]{2,1,0:T(8,128)(2,1)}), bf16[32,8,128]{2,1,0:T(8,128)(2,1)S(1)}, u32[]{:S(2)}, u32[]{:S(2)}) async-start(bf16[32,8,128]{2,1,0:T(8,128)(2,1)} %bitcast.6), calls=%async_computation | async-start | bytes 131072 | tf_op jit(solution)/shard_map/all_to_all | solution.py:250
  60.1 11.3 %all-to-all-start.1 = ((bf16[32,8,128]{2,1,0:T(8,128)(2,1)}), bf16[32,8,128]{2,1,0:T(8,128)(2,1)S(1)}, u32[]{:S(2)}, u32[]{:S(2)}) async-start(bf16[32,8,128]{2,1,0:T(8,128)(2,1)} %bitcast.35), calls=%async_computation.1 | async-start | bytes 131072 | tf_op jit(solution)/shard_map/all_to_all | solution.py:250
  72.3 21.5 %all-to-all-start.2 = ((bf16[8,2,16,1024]{3,2,1,0:T(8,128)(2,1)}), bf16[8,2,16,1024]{3,2,1,0:T(8,128)(2,1)S(1)}, u32[]{:S(2)}, u32[]{:S(2)}) async-start(bf16[8,2,16,1024]{3,2,1,0:T(8,128)(2,1)} %broadcast_in_dim.36), calls=%async_computation.2 | async-start | bytes 1048576 | tf_op jit(solution)/shard_map/all_to_all | solution.py:250
  93.8 0.8 copy-start
  108.7 20.5 %all-to-all-start.3 = ((bf16[8,2,16,1024]{3,2,1,0:T(8,128)(2,1)}), bf16[8,2,16,1024]{3,2,1,0:T(8,128)(2,1)S(1)}, u32[]{:S(2)}, u32[]{:S(2)}) async-start(bf16[8,2,16,1024]{3,2,1,0:T(8,128)(2,1)} %get-tuple-element.28), calls=%async_computation.3 | async-start | bytes 1048576 | tf_op jit(solution)/shard_map/all_to_all | solution.py:250
  112.8 92.7 %reduce-scatter.2.cloned.1.call-start = ((), (), s32[]{:S(2)}) async-start(), calls=%async_computation.7 | async-start | bytes 4718592 | tf_op jit(solution)/shard_map/reduce_scatter | solution.py:309
  167.4 5.0 %collective-permute-start.3 = (bf16[2,16,1024]{2,1,0:T(8,128)(2,1)S(1)}, bf16[2,16,1024]{2,1,0:T(8,128)(2,1)S(1)}, u32[]{:S(2)}, u32[]{:S(2)}) collective-permute-start(bf16[2,16,1024]{2,1,0:T(8,128)(2,1)S(1)} %bitcast.56), channel_id=1, source_target_pairs={{0,1},{2,3},{4,5},{6,7},{8,9},{10,11},{12,13},{14,15},{16,17},{18,... | collective-permute-start | bytes 196616 | tf_op jit(solution)/shard_map/ppermute | solution.py:270
  172.3 0.7 collective-permute-start.4
  173.1 0.7 collective-permute-start.5
Sparse Core Ops, SparseCore 0:
  10.4 58.8 all-gather.2
  138.8 66.7 reduce-scatter.1

commit v2 on v1

v2 whole, which is shorter than its diff:
```python
import functools

import jax
import jax.numpy as jnp
from jax import lax
from jax.experimental import pallas as pl
from jax.experimental.pallas import tpu as pltpu
from jax.sharding import PartitionSpec as P

HEAD = 128
GROUP = 8
KV_HEADS = 8
ROWS = 128
WIDE = GROUP * ROWS
TAIL = 128
PAIR = 256
LOG2E = 1.4426950408889634
SCALE = HEAD**-0.5
MASKED = -1e30
F32 = jnp.float32
BF16 = jnp.bfloat16
NT = (((1,), (1,)), ((), ()))
TN = (((0,), (0,)), ((), ()))
BLOCK = 512
PACK = 2
VMEM = 60 * 2**20


def dot(a, b, dims=(((1,), (0,)), ((), ()))):
    return lax.dot_general(a, b, dims, preferred_element_type=F32)


def fold(x, op):
    return op(x.reshape(x.shape[0] // 8, 8, x.shape[1]), axis=0)


def heads(ref):
    return jnp.concatenate([ref[:, g * HEAD : (g + 1) * HEAD] for g in range(PACK * GROUP)], axis=0)


SLICES = [(at // WIDE, slice(at % WIDE, at % WIDE + PAIR), slice(at, at + PAIR)) for at in range(0, PACK * WIDE, PAIR)]


def stagger(*stages):
    for step in range(len(SLICES) + len(stages) - 1):
        for late, stage in enumerate(stages):
            if 0 <= step - late < len(SLICES):
                stage(*SLICES[step - late])


def score(keys, q2, mask):
    return dot(keys, q2, NT) * (SCALE * LOG2E) + jnp.concatenate([mask, mask], axis=1)


def absorb(keys, values, mask, qs, stat, acc, s_ref, p_ref):
    size = keys[0].shape[0]
    kept = {}

    def scores(h, at, to):
        s = score(keys[h], qs[to], mask)
        s_ref[:size, to] = s
        top = jnp.max(fold(s, jnp.max), axis=0, keepdims=True)
        kept[to.start] = jnp.maximum(stat[h, 0:1, at], top)

    def weights(h, at, to):
        high = kept[to.start]
        p = jnp.exp2(s_ref[:size, to] - high)
        p_ref[:size, to] = p.astype(BF16)
        alpha = jnp.exp2(stat[h, 0:1, at] - high)
        stat[h, 0:1, at] = high
        stat[h, 1:2, at] = stat[h, 1:2, at] * alpha + jnp.sum(fold(p, jnp.sum), axis=0, keepdims=True)
        kept[to.start] = alpha

    def mix(h, at, to):
        acc[h, :, at] = acc[h, :, at] * kept[to.start] + dot(values[h], p_ref[:size, to], TN)

    stagger(scores, weights, mix)


def spread(keys, values, mask, qs, dos, stat, dq, s_ref, d_ref, p_ref, ds_ref):
    size = keys[0].shape[0]
    dk, dv = [0.0] * PACK, [0.0] * PACK

    def scores(h, at, to):
        s_ref[:size, to] = score(keys[h], qs[to], mask) - stat[h, 0:1, at]
        d_ref[:size, to] = dot(values[h], dos[to], NT) - stat[h, 1:2, at]

    def weights(h, at, to):
        p = jnp.exp2(s_ref[:size, to])
        p_ref[:size, to] = p.astype(BF16)
        ds_ref[:size, to] = (p * d_ref[:size, to]).astype(BF16)

    def mix(h, at, to):
        dk[h] = dk[h] + dot(ds_ref[:size, to], qs[to])
        dv[h] = dv[h] + dot(p_ref[:size, to], dos[to])
        dq[h, :, at] += dot(keys[h], ds_ref[:size, to], TN)

    stagger(scores, weights, mix)
    return [(x * SCALE).astype(BF16) for x in dk], [x.astype(BF16) for x in dv]


def lane(h):
    return slice(h * HEAD, (h + 1) * HEAD)


def blocks(span, near, bias, work):
    @pl.loop(span[0], span[1])
    def _(j):
        part = pl.ds(BLOCK // ROWS * j, BLOCK // ROWS)
        keys = [near[part, 0, :, lane(h)].reshape(BLOCK, HEAD) for h in range(PACK)]
        values = [near[part, 1, :, lane(h)].reshape(BLOCK, HEAD) for h in range(PACK)]
        work(part, keys, values, bias[pl.ds(pl.multiple_of(j * BLOCK, BLOCK), BLOCK)])


def near_fwd_body(span, bias, q_ref, near, stat, acc, qs, s_ref, p_ref):
    qs[...] = heads(q_ref)
    stat[:, 0:1] = jnp.full((PACK, 1, WIDE), MASKED, F32)
    stat[:, 1:2] = jnp.zeros((PACK, 1, WIDE), F32)
    acc[...] = jnp.zeros_like(acc)

    def work(part, keys, values, mask):
        absorb(keys, values, mask, qs, stat, acc, s_ref, p_ref)

    blocks(span, near, bias, work)


def tail(far, which):
    return [far[:, which, :, lane(h)].reshape(TAIL, HEAD) for h in range(PACK)]


def far_body(
    flag, bias, q_ref, do_ref, far, stat_in, acc_in, o_ref, stat_out, dq, dfar, qs, dos, stat, acc, s_ref, d_ref, p_ref, ds_ref
):
    stat[...] = stat_in[...]
    acc[...] = acc_in[...]
    dq[...] = jnp.zeros_like(dq)

    @pl.when(flag[0] > 0)
    def _():
        qs[...] = heads(q_ref)
        dos[...] = heads(do_ref)
        absorb(tail(far, 0), tail(far, 1), bias[...], qs, stat, acc, s_ref, p_ref)

    for h in range(PACK):
        norm = stat[h, 1:2]
        out = (acc[h] * (1.0 / norm)).astype(BF16)
        stat_out[h, 0:1] = stat[h, 0:1] + jnp.log2(norm)
        for g in range(GROUP):
            at, to = lane(g), lane(h * GROUP + g)
            o_ref[:, to] = out[:, at].T
            prod = do_ref[:, to].T.astype(F32) * out[:, at].astype(F32)
            stat_out[h, 1:2, at] = jnp.sum(prod, axis=0, keepdims=True)

    @pl.when(flag[0] > 0)
    def _():
        dk, dv = spread(
            tail(far, 0), tail(far, 1), bias[...], qs, dos, stat_out, dq, s_ref, d_ref, p_ref, ds_ref
        )
        for h in range(PACK):
            dfar[:, 0, :, lane(h)] = dk[h].reshape(8, 16, HEAD)
            dfar[:, 1, :, lane(h)] = dv[h].reshape(8, 16, HEAD)

    @pl.when(flag[0] == 0)
    def _():
        dfar[...] = jnp.zeros_like(dfar)


def near_bwd_body(span, bias, q_ref, do_ref, near, stat, dq_in, dq_ref, dnear, qs, dos, dq, s_ref, d_ref, p_ref, ds_ref):
    qs[...] = heads(q_ref)
    dos[...] = heads(do_ref)
    dq[...] = dq_in[...]
    dnear[...] = jnp.zeros_like(dnear)

    def work(part, keys, values, mask):
        dk, dv = spread(keys, values, mask, qs, dos, stat, dq, s_ref, d_ref, p_ref, ds_ref)
        for h in range(PACK):
            dnear[part, 0, :, lane(h)] = dk[h].reshape(BLOCK // ROWS, ROWS, HEAD)
            dnear[part, 1, :, lane(h)] = dv[h].reshape(BLOCK // ROWS, ROWS, HEAD)

    blocks(span, near, bias, work)
    for h in range(PACK):
        for g in range(GROUP):
            dq_ref[:, lane(h * GROUP + g)] = (dq[h, :, lane(g)] * SCALE).astype(BF16).T


def shape(dims, dtype=BF16):
    return jax.ShapeDtypeStruct(dims, dtype)


STAT = shape((KV_HEADS, 2, WIDE), F32)
ACC = shape((KV_HEADS, HEAD, WIDE), F32)
TALL = shape((PACK * WIDE, HEAD))


def spec(a):
    if len(a.shape) == 2:
        return pl.BlockSpec((ROWS, PACK * WIDE), lambda k: (0, k))
    if len(a.shape) == 4:
        return pl.BlockSpec(a.shape[:3] + (PACK * HEAD,), lambda k: (0, 0, 0, k))
    return pl.BlockSpec((PACK,) + a.shape[1:], lambda k: (k, 0, 0))


def call(body, scalars, bias, args, outs, scratch, keys, products):
    size = keys * WIDE * KV_HEADS
    return pl.pallas_call(
        body,
        grid=(KV_HEADS // PACK,),
        in_specs=[pl.BlockSpec(memory_space=pltpu.SMEM), pl.BlockSpec(bias.shape, lambda k: (0, 0))]
        + [spec(a) for a in args],
        out_specs=[spec(a) for a in outs],
        out_shape=outs,
        scratch_shapes=[pltpu.VMEM(a.shape, a.dtype) for a in scratch],
        compiler_params=pltpu.CompilerParams(vmem_limit_bytes=VMEM),
        cost_estimate=pl.CostEstimate(
            flops=4 * products * HEAD * size, bytes_accessed=16 * 2**20, transcendentals=size
        ),
    )(scalars, bias, *args)


ONE_STAT = shape((PACK, 2, WIDE), F32)
ONE_ACC = shape((PACK, HEAD, WIDE), F32)


def slabs(keys):
    wide = (keys, PACK * WIDE)
    return [shape(wide, F32), shape(wide, F32), shape(wide), shape(wide)]


def near_fwd(span, bias, q, near):
    scratch = [TALL, slabs(BLOCK)[0], slabs(BLOCK)[2]]
    return call(near_fwd_body, span, bias, [q, near], [STAT, ACC], scratch, 1024, 2)


def far_both(flag, bias, q, grad, far, stat, acc):
    outs = [shape(q.shape), STAT, ACC, shape(far.shape)]
    scratch = [TALL, TALL, ONE_STAT, ONE_ACC, *slabs(TAIL)]
    return call(far_body, flag, bias, [q, grad, far, stat, acc], outs, scratch, TAIL, 12)


def near_bwd(span, bias, q, grad, near, stat, dq):
    outs = [shape(q.shape), shape(near.shape)]
    scratch = [TALL, TALL, ONE_ACC, *slabs(BLOCK)]
    args = [q, grad, near, stat, dq]
    return call(near_bwd_body, span, bias, args, outs, scratch, 1024, 5)


def split(block):
    rows = block.shape[1] // 8
    return block.reshape(2, rows, 8, 8, HEAD).transpose(0, 1, 3, 2, 4).reshape(16 * rows, 8, HEAD)


def join(pieces):
    rows = pieces.shape[0] // 16
    return pieces.reshape(2, rows, 8, 8, HEAD).transpose(0, 1, 3, 2, 4).reshape(2, rows * 8, 1024)


def swap(pieces, axis):
    return lax.all_to_all(pieces, axis, split_axis=0, concat_axis=0, tiled=True)


def route(block, choose):
    pieces = swap(split(block), "dp").reshape(32, 8 * HEAD)
    pieces = jnp.dot(choose, pieces, preferred_element_type=F32).astype(BF16)
    return join(swap(pieces.reshape(32, 8, HEAD), "dp"))


def scatter_last(kv, z):
    half = lax.ppermute(kv[:, :64], "head", [(7, 3)])
    mine = jnp.where(z == 7, kv[:, 64:], half)
    send = jnp.where(z == 7, mine[:, :32], half[:, :32])
    quarter = lax.ppermute(send, "head", [(7, 5), (3, 1)])
    send = jnp.where(z % 4 == 3, mine[:, 32:48], quarter[:, :16])
    eighth = lax.ppermute(send, "head", [(7, 6), (5, 4), (3, 2), (1, 0)])
    return jnp.where(z % 2 == 0, eighth, jnp.where(z % 4 == 1, quarter[:, 16:], mine[:, 48:]))


def collect_last(piece):
    two = lax.ppermute(piece, "head", [(i, i + 1) for i in (0, 2, 4, 6)])
    two = jnp.concatenate([two, piece], axis=1)
    four = lax.ppermute(two, "head", [(1, 3), (5, 7)])
    four = jnp.concatenate([four, two], axis=1)
    eight = lax.ppermute(four, "head", [(3, 7)])
    return jnp.concatenate([eight, four], axis=1)


def per_device(queries, input_keys, input_values, output_gradient, doc_ids, spill_src, spill_len):
    rank, z = lax.axis_index("dp"), lax.axis_index("head")
    ids = jnp.arange(32, dtype=jnp.int32)
    kv = jnp.stack([input_keys, input_values])
    near = lax.all_gather(kv, "head", axis=0)

    wanted = (spill_src[:, None] == ids[None, :]).astype(BF16)
    piece = route(scatter_last(kv, z), wanted)
    near, piece = lax.optimization_barrier((near, piece))
    far = swap(jnp.broadcast_to(piece[None], (8, 2, 16, 1024)), "head")

    place = jnp.arange(1024, dtype=jnp.int32)
    row_at = z * ROWS + jnp.arange(ROWS, dtype=jnp.int32)
    row_docs = lax.dynamic_slice_in_dim(doc_ids, z * ROWS, ROWS)
    near_seen = (doc_ids[:, None] == row_docs[None, :]) & (place[:, None] <= row_at[None, :])
    far_seen = (place[:TAIL, None] >= TAIL - spill_len[rank]) & (row_docs[None, :] == 0)
    near_bias = jnp.where(near_seen, 0.0, MASKED).astype(F32)
    far_bias = jnp.where(far_seen, 0.0, MASKED).astype(F32)
    closing = doc_ids.reshape(8, ROWS)[:, ROWS - 1]
    begin = jnp.sum((closing < row_docs[0]).astype(jnp.int32))
    span = jnp.stack([begin // 4, z // 4 + 1])
    flag = (row_docs[:1] == 0).astype(jnp.int32)

    stat, acc = near_fwd(span, near_bias, queries, near)
    out, stat, dq, dfar = far_both(flag, far_bias, queries, output_gradient, far, stat, acc)
    parts = swap(dfar, "head")
    args = (span, near_bias, queries, output_gradient, near, stat, dq)
    dq, dnear = near_bwd(*args)
    dnear, parts = lax.optimization_barrier((dnear, parts))

    home = lax.psum_scatter(dnear, "head", scatter_dimension=0)
    piece = jnp.sum(parts.astype(F32), axis=0).astype(BF16)
    returned = collect_last(route(piece, wanted.T))
    totals = [
        (home[i].astype(F32) + jnp.where(z == 7, returned[i].astype(F32), 0.0)).astype(BF16) for i in range(2)
    ]
    return out, dq, *totals


def solution(mesh):
    rows = P(("dp", "head"), None)
    return jax.shard_map(
        per_device,
        mesh=mesh,
        in_specs=(rows, rows, rows, rows, P("dp"), P(), P()),
        out_specs=(rows, rows, rows, rows),
        check_vma=False,
    )
```

time: 218 us -> 207 us (0.950)
  Pallas kernels: 44.8 us -> 38.3 us
  blocking collectives: 28.3 us -> 25.3 us
    pallas_call x4 -> x3, Pallas kernels: 44.8 us -> 38.3 us  [call(): pl.pallas_call(body, grid=(KV_HEADS // PACK,), in_specs=[pl.BlockSpec(mem...]
    all_to_all x4, waiting for transfers between devices: 23 us -> 19.6 us  [swap(): return lax.all_to_all(pieces, axis, split_axis=0, concat_axis=0, tiled=True)]
    reduce_scatter x1, waiting for transfers between devices: 31.8 us -> 35 us  [per_device(): home = lax.psum_scatter(dnear, 'head', scatter_dimension=0)]
    all_to_all x2, blocking collectives: 28.3 us -> 25.3 us  [swap(): return lax.all_to_all(pieces, axis, split_axis=0, concat_axis=0, tiled=True)]
  transfers between devices with their start and end apart: 12 -> 12, of which waited for: 7 -> 7; matrix products, arithmetic and copies ran while one was open for 5% -> 5% of each run, Pallas kernels for 10% -> 13%
where the time goes in v2:
time: 207 us; the launch traced here: 204 us
  waiting for transfers between devices  80.1 us (39%)
  Pallas kernels  38.3 us (19%)
  starting transfers between devices  27.5 us (13%)
  blocking collectives  25.3 us (12%)
  between operations  17.6 us (9%)
  other arithmetic  11.3 us (5%)
  local copies, waits for them, and re-layouts  3.57 us (2%)
    pallas_call x3, Pallas kernels, call(): pl.pallas_call(body, grid=(KV_HEADS // PACK,), in_specs=[pl.BlockSpec(mem...  38.3 us
    reduce_scatter x1, waiting for transfers between devices, per_device(): home = lax.psum_scatter(dnear, 'head', scatter_dimension=0)  35 us
    all_to_all x2, blocking collectives, swap(): return lax.all_to_all(pieces, axis, split_axis=0, concat_axis=0, tiled=True)  25.3 us
    ppermute x1, waiting for transfers between devices, scatter_last(): eighth = lax.ppermute(send, 'head', [(7, 6), (5, 4), (3, 2), (1, 0)])  22.6 us
    all_to_all x4, starting transfers between devices, swap(): return lax.all_to_all(pieces, axis, split_axis=0, concat_axis=0, tiled=True)  21.3 us
    all_to_all x4, waiting for transfers between devices, swap(): return lax.all_to_all(pieces, axis, split_axis=0, concat_axis=0, tiled=True)  19.6 us
  transfers between devices with their start and end apart: 12, of which 7 were waited for; matrix products, arithmetic and copies ran while one was open for 5% of the time, Pallas kernels for 13%

profile of v2, /device:TPU:1, one launch (start us, length us, event | category | flops | bytes accessed | tf_op | source)
XLA Modules:
  0.0 204.2 jit_solution(10966050870596942500)
XLA Ops:
  7.2 0.0 copy-start.1
  7.2 0.0 copy-start.2
  7.2 0.0 all-gather.3.cloned.1.call-start
  7.2 1.9 pad_maximum_fusion
  9.1 0.0 all-gather.3.cloned.1.call-update
  9.1 1.0 fusion.8
  10.1 0.7 collective-permute-start
  10.8 1.2 dynamic_slice.7
  12.7 0.8 broadcast_compare_fusion
  13.5 0.0 collective-permute-done
  13.5 1.0 fusion.7
  14.5 0.7 collective-permute-start.1
  15.2 1.7 fusion.5.bias
  17.0 0.0 collective-permute-done.1
  17.0 1.3 collective-permute-start.2
  18.3 22.6 %collective-permute-done.2 = bf16[2,16,1024]{2,1,0:T(8,128)(2,1)S(1)} collective-permute-done((bf16[2,16,1024]{2,1,0:T(8,128)(2,1)S(1)}, bf16[2,16,1024]{2,1,0:T(8,128)(2,1)S(1)}, u32[]{:S(2)}, u32[]{:S(2)}) %collective-permute-start.2) | collective-permute-done | bytes 65568 | tf_op jit(solution)/shard_map/ppermute | solution.py:273
  40.9 0.6 fusion.13
  41.6 10.3 %all-to-all-start = ((bf16[32,8,128]{2,1,0:T(8,128)(2,1)}), bf16[32,8,128]{2,1,0:T(8,128)(2,1)S(1)}, u32[]{:S(2)}, u32[]{:S(2)}) async-start(bf16[32,8,128]{2,1,0:T(8,128)(2,1)} %bitcast.6), calls=%async_computation | async-start | bytes 131072 | tf_op jit(solution)/shard_map/all_to_all | solution.py:258
  51.9 0.7 and_select_fusion.bias
  52.6 6.6 %all-to-all-done = bf16[32,8,128]{2,1,0:T(8,128)(2,1)S(1)} async-done(((bf16[32,8,128]{2,1,0:T(8,128)(2,1)}), bf16[32,8,128]{2,1,0:T(8,128)(2,1)S(1)}, u32[]{:S(2)}, u32[]{:S(2)}) %all-to-all-start) | async-done | bytes 65568 | tf_op jit(solution)/shard_map/all_to_all | solution.py:258
  59.2 0.0 copy-done.2
  59.2 0.2 fusion
  59.4 0.7 copy.14
  60.1 3.9 %all-to-all-start.1 = ((bf16[32,8,128]{2,1,0:T(8,128)(2,1)}), bf16[32,8,128]{2,1,0:T(8,128)(2,1)S(1)}, u32[]{:S(2)}, u32[]{:S(2)}) async-start(bf16[32,8,128]{2,1,0:T(8,128)(2,1)} %bitcast.37), calls=%async_computation.1 | async-start | bytes 131072 | tf_op jit(solution)/shard_map/all_to_all | solution.py:258
  64.0 0.0 copy-done.1
  64.0 0.7 convert_reduce_fusion
  67.4 4.0 %all-to-all-done.1 = bf16[32,8,128]{2,1,0:T(8,128)(2,1)S(1)} async-done(((bf16[32,8,128]{2,1,0:T(8,128)(2,1)}), bf16[32,8,128]{2,1,0:T(8,128)(2,1)S(1)}, u32[]{:S(2)}, u32[]{:S(2)}) %all-to-all-start.1) | async-done | bytes 65568 | tf_op jit(solution)/shard_map/all_to_all | solution.py:258
  71.4 0.0 all-gather.3.cloned.1.call-done
  71.4 0.9 broadcast_in_dim.37
  72.3 3.6 %all-to-all-start.2 = ((bf16[8,2,16,1024]{3,2,1,0:T(8,128)(2,1)}), bf16[8,2,16,1024]{3,2,1,0:T(8,128)(2,1)S(1)}, u32[]{:S(2)}, u32[]{:S(2)}) async-start(bf16[8,2,16,1024]{3,2,1,0:T(8,128)(2,1)} %broadcast_in_dim.37), calls=%async_computation.2 | async-start | bytes 1048576 | tf_op jit(solution)/shard_map/all_to_all | solution.py:258
  75.9 0.6 pad_add_fusion.span
  76.5 10.1 %shard_map.102 = (f32[8,2,1024]{2,1,0:T(2,128)}, f32[8,128,1024]{2,1,0:T(8,128)}) custom-call(s32[2]{0:T(128)} %pad_add_fusion.span, f32[1024,128]{1,0:T(8,128)} %fusion.5.bias, bf16[128,8192]{1,0:T(8,128)(2,1)} %q_ref.5, bf16[8,2,128,1024]{3,2,1,0:T(8,128)(2,1)} %bitcast.75), custom_call_target="tpu_custom_call" | custom-call | flops 8589934592 | bytes 16777216 | tf_op jit(solution)/shard_map/pallas_call | solution.py:205
  86.6 7.2 %all-to-all-done.2.far = bf16[8,2,16,1024]{3,2,1,0:T(8,128)(2,1)S(1)} async-done(((bf16[8,2,16,1024]{3,2,1,0:T(8,128)(2,1)}), bf16[8,2,16,1024]{3,2,1,0:T(8,128)(2,1)S(1)}, u32[]{:S(2)}, u32[]{:S(2)}) %all-to-all-start.2) | async-done | bytes 524320 | tf_op jit(solution)/shard_map/all_to_all | solution.py:258
  93.8 0.0 copy-start
  93.8 0.8 copy-done
  94.6 12.1 %shard_map.103 = (bf16[128,8192]{1,0:T(8,128)(2,1)}, f32[8,2,1024]{2,1,0:T(2,128)}, f32[8,128,1024]{2,1,0:T(8,128)}, bf16[8,2,16,1024]{3,2,1,0:T(8,128)(2,1)}) custom-call(s32[1]{0:T(128)S(6)} %convert_element_type.42.flag, f32[128,128]{1,0:T(8,128)} %and_select_fusion.bias, bf16[128,8192]{1,0:T(8,128)(2,1)} %q_ref.5, bf16[128,8192]{1,0:T(8,128)(2,1)} %do_ref.3, ...), custom_call_target="tpu_custom_call" | custom-call | flops 6442450944 | bytes 16777216 | tf_op jit(solution)/shard_map/pallas_call | solution.py:205
  106.7 3.5 %all-to-all-start.3 = ((bf16[8,2,16,1024]{3,2,1,0:T(8,128)(2,1)}), bf16[8,2,16,1024]{3,2,1,0:T(8,128)(2,1)S(1)}, u32[]{:S(2)}, u32[]{:S(2)}) async-start(bf16[8,2,16,1024]{3,2,1,0:T(8,128)(2,1)} %get-tuple-element.25), calls=%async_computation.3 | async-start | bytes 1048576 | tf_op jit(solution)/shard_map/all_to_all | solution.py:258
  110.2 0.0 reduce-scatter.2.cloned.1.call-start
  110.3 16.0 %shard_map.104 = (bf16[128,8192]{1,0:T(8,128)(2,1)}, bf16[8,2,128,1024]{3,2,1,0:T(8,128)(2,1)}) custom-call(s32[2]{0:T(128)} %pad_add_fusion.span, f32[1024,128]{1,0:T(8,128)} %fusion.5.bias, bf16[128,8192]{1,0:T(8,128)(2,1)} %q_ref.5, bf16[128,8192]{1,0:T(8,128)(2,1)} %do_ref.3, bf16[8,2,128,1024]{3,2,1,0:T(8,128)(2,1)} %bitcast.76, ...), custom_call_target="tpu_custom_call" | custom-call | flops 21474836480 | bytes 16777216 | tf_op jit(solution)/shard_map/pallas_call | solution.py:205
  126.3 1.8 all-to-all-done.3
  128.1 0.0 reduce-scatter.2.cloned.1.call-update
  128.1 0.1 reduce_sum.22
  128.2 14.5 %all_to_all.30 = bf16[32,8,128]{2,1,0:T(8,128)(2,1)S(1)} all-to-all(bf16[32,8,128]{2,1,0:T(8,128)(2,1)S(1)} %bitcast.71), channel_id=1, replica_groups=mesh['dp'=32,'head'=8] {'dp'}, dimensions={0} | all-to-all | bytes 131072 | tf_op jit(solution)/shard_map/all_to_all | solution.py:258
  142.7 0.3 fusion.1
  143.0 10.9 %all_to_all.31 = bf16[32,8,128]{2,1,0:T(8,128)(2,1)S(1)} all-to-all(bf16[32,8,128]{2,1,0:T(8,128)(2,1)S(1)} %bitcast.70), channel_id=1, replica_groups=mesh['dp'=32,'head'=8] {'dp'}, dimensions={0} | all-to-all | bytes 131072 | tf_op jit(solution)/shard_map/all_to_all | solution.py:258
  153.8 2.2 %collective-permute-start.3 = (bf16[2,16,1024]{2,1,0:T(8,128)(2,1)S(1)}, bf16[2,16,1024]{2,1,0:T(8,128)(2,1)S(1)}, u32[]{:S(2)}, u32[]{:S(2)}) collective-permute-start(bf16[2,16,1024]{2,1,0:T(8,128)(2,1)S(1)} %bitcast.63), channel_id=1, source_target_pairs={{0,1},{2,3},{4,5},{6,7},{8,9},{10,11},{12,13},{14,15},{16,17},{18,... | collective-permute-start | bytes 196616 | tf_op jit(solution)/shard_map/ppermute | solution.py:278
  156.0 2.9 %collective-permute-done.3 = bf16[2,16,1024]{2,1,0:T(8,128)(2,1)S(1)} collective-permute-done((bf16[2,16,1024]{2,1,0:T(8,128)(2,1)S(1)}, bf16[2,16,1024]{2,1,0:T(8,128)(2,1)S(1)}, u32[]{:S(2)}, u32[]{:S(2)}) %collective-permute-start.3) | collective-permute-done | bytes 65568 | tf_op jit(solution)/shard_map/ppermute | solution.py:278
  158.9 0.7 collective-permute-start.4
  159.6 0.0 collective-permute-done.4
  159.6 0.7 collective-permute-start.5
  160.3 0.0 collective-permute-done.5
  160.4 35.0 %reduce-scatter.2.cloned.1.call-done = bf16[1,2,128,1024]{3,2,1,0:T(8,128)(2,1)} async-done(((bf16[8,2,128,1024]{3,2,1,0:T(8,128)(2,1)}), bf16[1,2,128,1024]{3,2,1,0:T(8,128)(2,1)}) %reduce-scatter.2.cloned.1.call-update) | async-done | bytes 524304 | tf_op jit(solution)/shard_map/reduce_scatter | solution.py:316
  195.4 2.0 fusion.2
  (9 shorter events, 0.1 us)
Async XLA Ops:
  7.2 56.9 %copy-start.1 = (s32[1024]{0:T(1024)S(1)}, s32[1024]{0:T(1024)}, u32[]{:S(2)}) copy-start(s32[1024]{0:T(1024)} %param.11) | copy-start | bytes 12292
  7.2 52.1 %copy-start.2 = (s32[32]{0:T(128)S(1)}, s32[32]{0:T(128)}, u32[]{:S(2)}) copy-start(s32[32]{0:T(128)} %param.12) | copy-start | bytes 388
  7.2 64.3 %all-gather.3.cloned.1.call-start = ((), (), s32[]{:S(2)}) async-start(), calls=%async_computation.8 | async-start | bytes 4718592 | tf_op jit(solution)/shard_map/all_gather | solution.py:290
  10.1 3.4 %collective-permute-start = (bf16[2,64,1024]{2,1,0:T(8,128)(2,1)S(1)}, bf16[2,64,1024]{2,1,0:T(8,128)(2,1)S(1)}, u32[]{:S(2)}, u32[]{:S(2)}) collective-permute-start(bf16[2,64,1024]{2,1,0:T(8,128)(2,1)S(1)} %fusion.8), channel_id=1, source_target_pairs={{7,3},{15,11},{23,19},{31,27},{39,35},{47,43},{55,51},{63,59},{71,... | collective-permute-start | bytes 786440 | tf_op jit(solution)/shard_map/ppermute | solution.py:268
  14.5 2.4 %collective-permute-start.1 = (bf16[2,32,1024]{2,1,0:T(8,128)(2,1)S(1)}, bf16[2,32,1024]{2,1,0:T(8,128)(2,1)S(1)}, u32[]{:S(2)}, u32[]{:S(2)}) collective-permute-start(bf16[2,32,1024]{2,1,0:T(8,128)(2,1)S(1)} %slice_select_fusion), channel_id=1, source_target_pairs={{7,5},{3,1},{15,13},{11,9},{23,21},{19,17},{31,29},{27,25},{39,37}... | collective-permute-start | bytes 393224 | tf_op jit(solution)/shard_map/ppermute | solution.py:271
  17.0 24.0 %collective-permute-start.2 = (bf16[2,16,1024]{2,1,0:T(8,128)(2,1)S(1)}, bf16[2,16,1024]{2,1,0:T(8,128)(2,1)S(1)}, u32[]{:S(2)}, u32[]{:S(2)}) collective-permute-start(bf16[2,16,1024]{2,1,0:T(8,128)(2,1)S(1)} %slice_select_fusion.2), channel_id=1, source_target_pairs={{7,6},{5,4},{3,2},{1,0},{15,14},{13,12},{11,10},{9,8},{23,22},{21,... | collective-permute-start | bytes 196616 | tf_op jit(solution)/shard_map/ppermute | solution.py:273
  41.6 17.7 %all-to-all-start = ((bf16[32,8,128]{2,1,0:T(8,128)(2,1)}), bf16[32,8,128]{2,1,0:T(8,128)(2,1)S(1)}, u32[]{:S(2)}, u32[]{:S(2)}) async-start(bf16[32,8,128]{2,1,0:T(8,128)(2,1)} %bitcast.6), calls=%async_computation | async-start | bytes 131072 | tf_op jit(solution)/shard_map/all_to_all | solution.py:258
  60.1 11.3 %all-to-all-start.1 = ((bf16[32,8,128]{2,1,0:T(8,128)(2,1)}), bf16[32,8,128]{2,1,0:T(8,128)(2,1)S(1)}, u32[]{:S(2)}, u32[]{:S(2)}) async-start(bf16[32,8,128]{2,1,0:T(8,128)(2,1)} %bitcast.37), calls=%async_computation.1 | async-start | bytes 131072 | tf_op jit(solution)/shard_map/all_to_all | solution.py:258
  72.3 21.5 %all-to-all-start.2 = ((bf16[8,2,16,1024]{3,2,1,0:T(8,128)(2,1)}), bf16[8,2,16,1024]{3,2,1,0:T(8,128)(2,1)S(1)}, u32[]{:S(2)}, u32[]{:S(2)}) async-start(bf16[8,2,16,1024]{3,2,1,0:T(8,128)(2,1)} %broadcast_in_dim.37), calls=%async_computation.2 | async-start | bytes 1048576 | tf_op jit(solution)/shard_map/all_to_all | solution.py:258
  93.8 0.8 copy-start
  106.7 21.4 %all-to-all-start.3 = ((bf16[8,2,16,1024]{3,2,1,0:T(8,128)(2,1)}), bf16[8,2,16,1024]{3,2,1,0:T(8,128)(2,1)S(1)}, u32[]{:S(2)}, u32[]{:S(2)}) async-start(bf16[8,2,16,1024]{3,2,1,0:T(8,128)(2,1)} %get-tuple-element.25), calls=%async_computation.3 | async-start | bytes 1048576 | tf_op jit(solution)/shard_map/all_to_all | solution.py:258
  110.2 85.1 %reduce-scatter.2.cloned.1.call-start = ((), (), s32[]{:S(2)}) async-start(), calls=%async_computation.7 | async-start | bytes 4718592 | tf_op jit(solution)/shard_map/reduce_scatter | solution.py:316
  153.8 5.1 %collective-permute-start.3 = (bf16[2,16,1024]{2,1,0:T(8,128)(2,1)S(1)}, bf16[2,16,1024]{2,1,0:T(8,128)(2,1)S(1)}, u32[]{:S(2)}, u32[]{:S(2)}) collective-permute-start(bf16[2,16,1024]{2,1,0:T(8,128)(2,1)S(1)} %bitcast.63), channel_id=1, source_target_pairs={{0,1},{2,3},{4,5},{6,7},{8,9},{10,11},{12,13},{14,15},{16,17},{18,... | collective-permute-start | bytes 196616 | tf_op jit(solution)/shard_map/ppermute | solution.py:278
  158.9 0.7 collective-permute-start.4
  159.6 0.7 collective-permute-start.5
Sparse Core Ops, SparseCore 0:
  10.4 58.8 all-gather.2
  128.2 67.0 reduce-scatter.1

commit v3 on v2

--- a/solution.py
+++ b/solution.py
@@ -21,7 +21,7 @@
 BF16 = jnp.bfloat16
 NT = (((1,), (1,)), ((), ()))
 TN = (((0,), (0,)), ((), ()))
-BLOCK = 512
+KEYS = 1024
 PACK = 2
 VMEM = 60 * 2**20
 
@@ -103,25 +103,17 @@
     return slice(h * HEAD, (h + 1) * HEAD)
 
 
-def blocks(span, near, bias, work):
-    @pl.loop(span[0], span[1])
-    def _(j):
-        part = pl.ds(BLOCK // ROWS * j, BLOCK // ROWS)
-        keys = [near[part, 0, :, lane(h)].reshape(BLOCK, HEAD) for h in range(PACK)]
-        values = [near[part, 1, :, lane(h)].reshape(BLOCK, HEAD) for h in range(PACK)]
-        work(part, keys, values, bias[pl.ds(pl.multiple_of(j * BLOCK, BLOCK), BLOCK)])
-
-
-def near_fwd_body(span, bias, q_ref, near, stat, acc, qs, s_ref, p_ref):
+def chunk(near, which):
+    return [near[:, which, :, lane(h)].reshape(KEYS, HEAD) for h in range(PACK)]
+
+
+def near_fwd_body(bias, q_ref, near, stat, acc, qs, s_ref, p_ref):
     qs[...] = heads(q_ref)
     stat[:, 0:1] = jnp.full((PACK, 1, WIDE), MASKED, F32)
     stat[:, 1:2] = jnp.zeros((PACK, 1, WIDE), F32)
     acc[...] = jnp.zeros_like(acc)
 
-    def work(part, keys, values, mask):
-        absorb(keys, values, mask, qs, stat, acc, s_ref, p_ref)
-
-    blocks(span, near, bias, work)
+    absorb(chunk(near, 0), chunk(near, 1), bias[...], qs, stat, acc, s_ref, p_ref)
 
 
 def tail(far, which):
@@ -165,19 +157,14 @@
         dfar[...] = jnp.zeros_like(dfar)
 
 
-def near_bwd_body(span, bias, q_ref, do_ref, near, stat, dq_in, dq_ref, dnear, qs, dos, dq, s_ref, d_ref, p_ref, ds_ref):
+def near_bwd_body(bias, q_ref, do_ref, near, stat, dq_in, dq_ref, dnear, qs, dos, dq, s_ref, d_ref, p_ref, ds_ref):
     qs[...] = heads(q_ref)
     dos[...] = heads(do_ref)
     dq[...] = dq_in[...]
-    dnear[...] = jnp.zeros_like(dnear)
-
-    def work(part, keys, values, mask):
-        dk, dv = spread(keys, values, mask, qs, dos, stat, dq, s_ref, d_ref, p_ref, ds_ref)
-        for h in range(PACK):
-            dnear[part, 0, :, lane(h)] = dk[h].reshape(BLOCK // ROWS, ROWS, HEAD)
-            dnear[part, 1, :, lane(h)] = dv[h].reshape(BLOCK // ROWS, ROWS, HEAD)
-
-    blocks(span, near, bias, work)
+    dk, dv = spread(chunk(near, 0), chunk(near, 1), bias[...], qs, dos, stat, dq, s_ref, d_ref, p_ref, ds_ref)
+    for h in range(PACK):
+        dnear[:, 0, :, lane(h)] = dk[h].reshape(8, ROWS, HEAD)
+        dnear[:, 1, :, lane(h)] = dv[h].reshape(8, ROWS, HEAD)
     for h in range(PACK):
         for g in range(GROUP):
             dq_ref[:, lane(h * GROUP + g)] = (dq[h, :, lane(g)] * SCALE).astype(BF16).T
@@ -200,12 +187,13 @@
     return pl.BlockSpec((PACK,) + a.shape[1:], lambda k: (k, 0, 0))
 
 
-def call(body, scalars, bias, args, outs, scratch, keys, products):
+def call(body, lead, args, outs, scratch, keys, products):
     size = keys * WIDE * KV_HEADS
     return pl.pallas_call(
         body,
         grid=(KV_HEADS // PACK,),
-        in_specs=[pl.BlockSpec(memory_space=pltpu.SMEM), pl.BlockSpec(bias.shape, lambda k: (0, 0))]
+        in_specs=[pl.BlockSpec(memory_space=pltpu.SMEM) for a in lead[:-1]]
+        + [pl.BlockSpec(lead[-1].shape, lambda k: (0, 0))]
         + [spec(a) for a in args],
         out_specs=[spec(a) for a in outs],
         out_shape=outs,
@@ -214,7 +202,7 @@
         cost_estimate=pl.CostEstimate(
             flops=4 * products * HEAD * size, bytes_accessed=16 * 2**20, transcendentals=size
         ),
-    )(scalars, bias, *args)
+    )(*lead, *args)
 
 
 ONE_STAT = shape((PACK, 2, WIDE), F32)
@@ -226,22 +214,22 @@
     return [shape(wide, F32), shape(wide, F32), shape(wide), shape(wide)]
 
 
-def near_fwd(span, bias, q, near):
-    scratch = [TALL, slabs(BLOCK)[0], slabs(BLOCK)[2]]
-    return call(near_fwd_body, span, bias, [q, near], [STAT, ACC], scratch, 1024, 2)
+def near_fwd(bias, q, near):
+    scratch = [TALL, slabs(KEYS)[0], slabs(KEYS)[2]]
+    return call(near_fwd_body, [bias], [q, near], [STAT, ACC], scratch, 1024, 2)
 
 
 def far_both(flag, bias, q, grad, far, stat, acc):
     outs = [shape(q.shape), STAT, ACC, shape(far.shape)]
     scratch = [TALL, TALL, ONE_STAT, ONE_ACC, *slabs(TAIL)]
-    return call(far_body, flag, bias, [q, grad, far, stat, acc], outs, scratch, TAIL, 12)
-
-
-def near_bwd(span, bias, q, grad, near, stat, dq):
+    return call(far_body, [flag, bias], [q, grad, far, stat, acc], outs, scratch, TAIL, 12)
+
+
+def near_bwd(bias, q, grad, near, stat, dq):
     outs = [shape(q.shape), shape(near.shape)]
-    scratch = [TALL, TALL, ONE_ACC, *slabs(BLOCK)]
+    scratch = [TALL, TALL, ONE_ACC, *slabs(KEYS)]
     args = [q, grad, near, stat, dq]
-    return call(near_bwd_body, span, bias, args, outs, scratch, 1024, 5)
+    return call(near_bwd_body, [bias], args, outs, scratch, 1024, 5)
 
 
 def split(block):
@@ -301,15 +289,12 @@
     far_seen = (place[:TAIL, None] >= TAIL - spill_len[rank]) & (row_docs[None, :] == 0)
     near_bias = jnp.where(near_seen, 0.0, MASKED).astype(F32)
     far_bias = jnp.where(far_seen, 0.0, MASKED).astype(F32)
-    closing = doc_ids.reshape(8, ROWS)[:, ROWS - 1]
-    begin = jnp.sum((closing < row_docs[0]).astype(jnp.int32))
-    span = jnp.stack([begin // 4, z // 4 + 1])
     flag = (row_docs[:1] == 0).astype(jnp.int32)
 
-    stat, acc = near_fwd(span, near_bias, queries, near)
+    stat, acc = near_fwd(near_bias, queries, near)
     out, stat, dq, dfar = far_both(flag, far_bias, queries, output_gradient, far, stat, acc)
     parts = swap(dfar, "head")
-    args = (span, near_bias, queries, output_gradient, near, stat, dq)
+    args = (near_bias, queries, output_gradient, near, stat, dq)
     dq, dnear = near_bwd(*args)
     dnear, parts = lax.optimization_barrier((dnear, parts))
 

time: 207 us -> 205 us (level)
  Pallas kernels: 38.3 us -> 52 us
  waiting for transfers between devices: 80.1 us -> 68.5 us
  between operations: 17.6 us -> 15 us
    pallas_call x3, Pallas kernels: 38.3 us -> 52 us  [call(): pl.pallas_call(body, grid=(KV_HEADS // PACK,), in_specs=[pl.BlockSpec(mem...]
    reduce_scatter x1, waiting for transfers between devices: 35 us -> 25.1 us  [per_device(): home = lax.psum_scatter(dnear, 'head', scatter_dimension=0)]
    all_to_all x4, waiting for transfers between devices: 19.6 us -> 14.3 us  [swap(): return lax.all_to_all(pieces, axis, split_axis=0, concat_axis=0, tiled=True)]
    ppermute x1, waiting for transfers between devices: 22.6 us -> 26.3 us  [scatter_last(): eighth = lax.ppermute(send, 'head', [(7, 6), (5, 4), (3, 2), (1, 0)])]
  transfers between devices with their start and end apart: 12 -> 12, of which waited for: 7 -> 6; matrix products, arithmetic and copies ran while one was open for 5% -> 4% of each run, Pallas kernels for 13% -> 20%
where the time goes in v3:
time: 205 us; the launch traced here: 202 us
  waiting for transfers between devices  68.5 us (33%)
  Pallas kernels  52 us (25%)
  starting transfers between devices  28.8 us (14%)
  blocking collectives  25.3 us (12%)
  between operations  15 us (7%)
  other arithmetic  9.27 us (5%)
  local copies, waits for them, and re-layouts  2.91 us (1%)
    pallas_call x3, Pallas kernels, call(): pl.pallas_call(body, grid=(KV_HEADS // PACK,), in_specs=[pl.BlockSpec(mem...  52 us
    ppermute x1, waiting for transfers between devices, scatter_last(): eighth = lax.ppermute(send, 'head', [(7, 6), (5, 4), (3, 2), (1, 0)])  26.3 us
    all_to_all x2, blocking collectives, swap(): return lax.all_to_all(pieces, axis, split_axis=0, concat_axis=0, tiled=True)  25.3 us
    reduce_scatter x1, waiting for transfers between devices, per_device(): home = lax.psum_scatter(dnear, 'head', scatter_dimension=0)  25.1 us
    all_to_all x4, starting transfers between devices, swap(): return lax.all_to_all(pieces, axis, split_axis=0, concat_axis=0, tiled=True)  21.3 us
    all_to_all x4, waiting for transfers between devices, swap(): return lax.all_to_all(pieces, axis, split_axis=0, concat_axis=0, tiled=True)  14.3 us
  transfers between devices with their start and end apart: 12, of which 6 were waited for; matrix products, arithmetic and copies ran while one was open for 4% of the time, Pallas kernels for 20%

profile of v3, /device:TPU:1, one launch (start us, length us, event | category | flops | bytes accessed | tf_op | source)
XLA Modules:
  0.0 202.2 jit_solution(15769657891887815124)
XLA Ops:
  7.2 0.0 copy-start.1
  7.2 0.0 copy-start.3
  7.2 0.0 copy-start.2
  7.2 0.0 all-gather.3.cloned.1.call-start
  7.2 1.9 pad_maximum_fusion
  9.1 0.0 all-gather.3.cloned.1.call-update
  9.1 1.0 fusion.8
  10.1 0.7 collective-permute-start
  10.8 0.0 collective-permute-done
  10.8 1.0 fusion.7
  11.9 0.7 collective-permute-start.1
  12.6 0.8 broadcast_compare_fusion
  13.3 0.0 collective-permute-done.1
  13.4 1.3 collective-permute-start.2
  14.7 26.3 %collective-permute-done.2 = bf16[2,16,1024]{2,1,0:T(8,128)(2,1)S(1)} collective-permute-done((bf16[2,16,1024]{2,1,0:T(8,128)(2,1)S(1)}, bf16[2,16,1024]{2,1,0:T(8,128)(2,1)S(1)}, u32[]{:S(2)}, u32[]{:S(2)}) %collective-permute-start.2) | collective-permute-done | bytes 65568 | tf_op jit(solution)/shard_map/ppermute | solution.py:261
  40.9 0.6 fusion.13
  41.6 10.3 %all-to-all-start = ((bf16[32,8,128]{2,1,0:T(8,128)(2,1)}), bf16[32,8,128]{2,1,0:T(8,128)(2,1)S(1)}, u32[]{:S(2)}, u32[]{:S(2)}) async-start(bf16[32,8,128]{2,1,0:T(8,128)(2,1)} %bitcast.6), calls=%async_computation | async-start | bytes 131072 | tf_op jit(solution)/shard_map/all_to_all | solution.py:246
  51.9 0.0 copy-done.1
  51.9 1.1 fusion.5.bias
  53.0 0.0 copy-done.3
  53.0 0.6 dynamic_slice.7
  54.2 5.0 %all-to-all-done = bf16[32,8,128]{2,1,0:T(8,128)(2,1)S(1)} async-done(((bf16[32,8,128]{2,1,0:T(8,128)(2,1)}), bf16[32,8,128]{2,1,0:T(8,128)(2,1)S(1)}, u32[]{:S(2)}, u32[]{:S(2)}) %all-to-all-start) | async-done | bytes 65568 | tf_op jit(solution)/shard_map/all_to_all | solution.py:246
  59.3 0.0 copy-done.2
  59.3 0.2 fusion
  59.5 0.7 copy.12
  60.1 3.9 %all-to-all-start.1 = ((bf16[32,8,128]{2,1,0:T(8,128)(2,1)}), bf16[32,8,128]{2,1,0:T(8,128)(2,1)S(1)}, u32[]{:S(2)}, u32[]{:S(2)}) async-start(bf16[32,8,128]{2,1,0:T(8,128)(2,1)} %bitcast.33), calls=%async_computation.1 | async-start | bytes 131072 | tf_op jit(solution)/shard_map/all_to_all | solution.py:246
  64.0 7.4 %all-to-all-done.1 = bf16[32,8,128]{2,1,0:T(8,128)(2,1)S(1)} async-done(((bf16[32,8,128]{2,1,0:T(8,128)(2,1)}), bf16[32,8,128]{2,1,0:T(8,128)(2,1)S(1)}, u32[]{:S(2)}, u32[]{:S(2)}) %all-to-all-start.1) | async-done | bytes 65568 | tf_op jit(solution)/shard_map/all_to_all | solution.py:246
  71.5 0.0 all-gather.3.cloned.1.call-done
  71.5 0.9 broadcast_in_dim.37
  72.3 3.6 %all-to-all-start.2 = ((bf16[8,2,16,1024]{3,2,1,0:T(8,128)(2,1)}), bf16[8,2,16,1024]{3,2,1,0:T(8,128)(2,1)S(1)}, u32[]{:S(2)}, u32[]{:S(2)}) async-start(bf16[8,2,16,1024]{3,2,1,0:T(8,128)(2,1)} %broadcast_in_dim.37), calls=%async_computation.2 | async-start | bytes 1048576 | tf_op jit(solution)/shard_map/all_to_all | solution.py:246
  75.9 0.7 and_select_fusion.bias
  76.6 15.4 %shard_map.102 = (f32[8,2,1024]{2,1,0:T(2,128)}, f32[8,128,1024]{2,1,0:T(8,128)}) custom-call(f32[1024,128]{1,0:T(8,128)} %fusion.5.bias, bf16[128,8192]{1,0:T(8,128)(2,1)} %q_ref.5, bf16[8,2,128,1024]{3,2,1,0:T(8,128)(2,1)} %bitcast.69), custom_call_target="tpu_custom_call" | custom-call | flops 8589934592 | bytes 16777216 | tf_op jit(solution)/shard_map/pallas_call | solution.py:192
  92.0 1.8 all-to-all-done.2.far
  93.8 0.0 copy-start
  93.8 0.8 copy-done
  94.6 12.1 %shard_map.103 = (bf16[128,8192]{1,0:T(8,128)(2,1)}, f32[8,2,1024]{2,1,0:T(2,128)}, f32[8,128,1024]{2,1,0:T(8,128)}, bf16[8,2,16,1024]{3,2,1,0:T(8,128)(2,1)}) custom-call(s32[1]{0:T(128)S(6)} %convert_element_type.38.flag, f32[128,128]{1,0:T(8,128)} %and_select_fusion.bias, bf16[128,8192]{1,0:T(8,128)(2,1)} %q_ref.5, bf16[128,8192]{1,0:T(8,128)(2,1)} %do_ref.3, ...), custom_call_target="tpu_custom_call" | custom-call | flops 6442450944 | bytes 16777216 | tf_op jit(solution)/shard_map/pallas_call | solution.py:192
  106.7 3.5 %all-to-all-start.3 = ((bf16[8,2,16,1024]{3,2,1,0:T(8,128)(2,1)}), bf16[8,2,16,1024]{3,2,1,0:T(8,128)(2,1)S(1)}, u32[]{:S(2)}, u32[]{:S(2)}) async-start(bf16[8,2,16,1024]{3,2,1,0:T(8,128)(2,1)} %get-tuple-element.25), calls=%async_computation.3 | async-start | bytes 1048576 | tf_op jit(solution)/shard_map/all_to_all | solution.py:246
  110.2 0.2 reduce-scatter.2.cloned.1.call-start
  110.5 24.5 %shard_map.104 = (bf16[128,8192]{1,0:T(8,128)(2,1)}, bf16[8,2,128,1024]{3,2,1,0:T(8,128)(2,1)}) custom-call(f32[1024,128]{1,0:T(8,128)} %fusion.5.bias, bf16[128,8192]{1,0:T(8,128)(2,1)} %q_ref.5, bf16[128,8192]{1,0:T(8,128)(2,1)} %do_ref.3, bf16[8,2,128,1024]{3,2,1,0:T(8,128)(2,1)} %bitcast.70, f32[8,2,1024]{2,1,0:T(2,128)} %get-tuple-element.21.stat, ...), custom_call_target="tpu_custom_call" | custom-call | flops 21474836480 | bytes 16777216 | tf_op jit(solution)/shard_map/pallas_call | solution.py:192
  135.0 0.0 all-to-all-done.3
  135.0 0.0 reduce-scatter.2.cloned.1.call-update
  135.0 0.1 reduce_sum.12
  135.1 14.5 %all_to_all.30 = bf16[32,8,128]{2,1,0:T(8,128)(2,1)S(1)} all-to-all(bf16[32,8,128]{2,1,0:T(8,128)(2,1)S(1)} %bitcast.67), channel_id=1, replica_groups=mesh['dp'=32,'head'=8] {'dp'}, dimensions={0} | all-to-all | bytes 131072 | tf_op jit(solution)/shard_map/all_to_all | solution.py:246
  149.6 0.3 fusion.1
  149.9 10.9 %all_to_all.31 = bf16[32,8,128]{2,1,0:T(8,128)(2,1)S(1)} all-to-all(bf16[32,8,128]{2,1,0:T(8,128)(2,1)S(1)} %bitcast.66), channel_id=1, replica_groups=mesh['dp'=32,'head'=8] {'dp'}, dimensions={0} | all-to-all | bytes 131072 | tf_op jit(solution)/shard_map/all_to_all | solution.py:246
  160.7 3.3 %collective-permute-start.3 = (bf16[2,16,1024]{2,1,0:T(8,128)(2,1)S(1)}, bf16[2,16,1024]{2,1,0:T(8,128)(2,1)S(1)}, u32[]{:S(2)}, u32[]{:S(2)}) collective-permute-start(bf16[2,16,1024]{2,1,0:T(8,128)(2,1)S(1)} %bitcast.59), channel_id=1, source_target_pairs={{0,1},{2,3},{4,5},{6,7},{8,9},{10,11},{12,13},{14,15},{16,17},{18,... | collective-permute-start | bytes 196616 | tf_op jit(solution)/shard_map/ppermute | solution.py:266
  164.0 2.8 %collective-permute-done.3 = bf16[2,16,1024]{2,1,0:T(8,128)(2,1)S(1)} collective-permute-done((bf16[2,16,1024]{2,1,0:T(8,128)(2,1)S(1)}, bf16[2,16,1024]{2,1,0:T(8,128)(2,1)S(1)}, u32[]{:S(2)}, u32[]{:S(2)}) %collective-permute-start.3) | collective-permute-done | bytes 65568 | tf_op jit(solution)/shard_map/ppermute | solution.py:266
  166.9 0.7 collective-permute-start.4
  167.5 0.0 collective-permute-done.4
  167.6 0.7 collective-permute-start.5
  168.3 0.0 collective-permute-done.5
  168.3 25.1 %reduce-scatter.2.cloned.1.call-done = bf16[1,2,128,1024]{3,2,1,0:T(8,128)(2,1)} async-done(((bf16[8,2,128,1024]{3,2,1,0:T(8,128)(2,1)}), bf16[1,2,128,1024]{3,2,1,0:T(8,128)(2,1)}) %reduce-scatter.2.cloned.1.call-update) | async-done | bytes 524304 | tf_op jit(solution)/shard_map/reduce_scatter | solution.py:301
  193.4 2.0 fusion.2
  (9 shorter events, 0.1 us)
Async XLA Ops:
  7.2 44.8 %copy-start.1 = (s32[1024]{0:T(1024)S(1)}, s32[1024]{0:T(1024)}, u32[]{:S(2)}) copy-start(s32[1024]{0:T(1024)} %param.11) | copy-start | bytes 12292
  7.2 45.8 %copy-start.3 = (s32[32]{0:T(128)S(1)}, s32[32]{0:T(128)}, u32[]{:S(2)}) copy-start(s32[32]{0:T(128)} %param.13) | copy-start | bytes 388
  7.2 52.1 %copy-start.2 = (s32[32]{0:T(128)S(1)}, s32[32]{0:T(128)}, u32[]{:S(2)}) copy-start(s32[32]{0:T(128)} %param.12) | copy-start | bytes 388
  7.2 64.3 %all-gather.3.cloned.1.call-start = ((), (), s32[]{:S(2)}) async-start(), calls=%async_computation.8 | async-start | bytes 4718592 | tf_op jit(solution)/shard_map/all_gather | solution.py:278
  10.1 0.7 collective-permute-start
  11.9 1.5 collective-permute-start.1
  13.4 27.6 %collective-permute-start.2 = (bf16[2,16,1024]{2,1,0:T(8,128)(2,1)S(1)}, bf16[2,16,1024]{2,1,0:T(8,128)(2,1)S(1)}, u32[]{:S(2)}, u32[]{:S(2)}) collective-permute-start(bf16[2,16,1024]{2,1,0:T(8,128)(2,1)S(1)} %slice_select_fusion.2), channel_id=1, source_target_pairs={{7,6},{5,4},{3,2},{1,0},{15,14},{13,12},{11,10},{9,8},{23,22},{21,... | collective-permute-start | bytes 196616 | tf_op jit(solution)/shard_map/ppermute | solution.py:261
  41.6 17.7 %all-to-all-start = ((bf16[32,8,128]{2,1,0:T(8,128)(2,1)}), bf16[32,8,128]{2,1,0:T(8,128)(2,1)S(1)}, u32[]{:S(2)}, u32[]{:S(2)}) async-start(bf16[32,8,128]{2,1,0:T(8,128)(2,1)} %bitcast.6), calls=%async_computation | async-start | bytes 131072 | tf_op jit(solution)/shard_map/all_to_all | solution.py:246
  60.1 11.3 %all-to-all-start.1 = ((bf16[32,8,128]{2,1,0:T(8,128)(2,1)}), bf16[32,8,128]{2,1,0:T(8,128)(2,1)S(1)}, u32[]{:S(2)}, u32[]{:S(2)}) async-start(bf16[32,8,128]{2,1,0:T(8,128)(2,1)} %bitcast.33), calls=%async_computation.1 | async-start | bytes 131072 | tf_op jit(solution)/shard_map/all_to_all | solution.py:246
  72.3 21.5 %all-to-all-start.2 = ((bf16[8,2,16,1024]{3,2,1,0:T(8,128)(2,1)}), bf16[8,2,16,1024]{3,2,1,0:T(8,128)(2,1)S(1)}, u32[]{:S(2)}, u32[]{:S(2)}) async-start(bf16[8,2,16,1024]{3,2,1,0:T(8,128)(2,1)} %broadcast_in_dim.37), calls=%async_computation.2 | async-start | bytes 1048576 | tf_op jit(solution)/shard_map/all_to_all | solution.py:246
  93.8 0.8 copy-start
  106.7 28.2 %all-to-all-start.3 = ((bf16[8,2,16,1024]{3,2,1,0:T(8,128)(2,1)}), bf16[8,2,16,1024]{3,2,1,0:T(8,128)(2,1)S(1)}, u32[]{:S(2)}, u32[]{:S(2)}) async-start(bf16[8,2,16,1024]{3,2,1,0:T(8,128)(2,1)} %get-tuple-element.25), calls=%async_computation.3 | async-start | bytes 1048576 | tf_op jit(solution)/shard_map/all_to_all | solution.py:246
  110.2 83.1 %reduce-scatter.2.cloned.1.call-start = ((), (), s32[]{:S(2)}) async-start(), calls=%async_computation.7 | async-start | bytes 4718592 | tf_op jit(solution)/shard_map/reduce_scatter | solution.py:301
  160.7 6.1 %collective-permute-start.3 = (bf16[2,16,1024]{2,1,0:T(8,128)(2,1)S(1)}, bf16[2,16,1024]{2,1,0:T(8,128)(2,1)S(1)}, u32[]{:S(2)}, u32[]{:S(2)}) collective-permute-start(bf16[2,16,1024]{2,1,0:T(8,128)(2,1)S(1)} %bitcast.59), channel_id=1, source_target_pairs={{0,1},{2,3},{4,5},{6,7},{8,9},{10,11},{12,13},{14,15},{16,17},{18,... | collective-permute-start | bytes 196616 | tf_op jit(solution)/shard_map/ppermute | solution.py:266
  166.9 0.7 collective-permute-start.4
  167.6 0.7 collective-permute-start.5
Sparse Core Ops, SparseCore 0:
  10.4 58.8 all-gather.2
  135.1 58.2 reduce-scatter.1

commit v4 on v3

--- a/solution.py
+++ b/solution.py
@@ -274,12 +274,11 @@
 def per_device(queries, input_keys, input_values, output_gradient, doc_ids, spill_src, spill_len):
     rank, z = lax.axis_index("dp"), lax.axis_index("head")
     ids = jnp.arange(32, dtype=jnp.int32)
-    kv = jnp.stack([input_keys, input_values])
+    kv = lax.optimization_barrier(jnp.stack([input_keys, input_values]))
     near = lax.all_gather(kv, "head", axis=0)
 
     wanted = (spill_src[:, None] == ids[None, :]).astype(BF16)
     piece = route(scatter_last(kv, z), wanted)
-    near, piece = lax.optimization_barrier((near, piece))
     far = swap(jnp.broadcast_to(piece[None], (8, 2, 16, 1024)), "head")
 
     place = jnp.arange(1024, dtype=jnp.int32)

time: 205 us -> 202 us (0.985)
  blocking collectives: 25.3 us -> 23 us
    all_to_all x2, blocking collectives: 25.3 us -> 23 us  [swap(): return lax.all_to_all(pieces, axis, split_axis=0, concat_axis=0, tiled=True)]
where the time goes in v4:
time: 202 us; the launch traced here: 200 us
  waiting for transfers between devices  67.8 us (34%)
  Pallas kernels  52 us (26%)
  starting transfers between devices  28.8 us (14%)
  blocking collectives  23 us (11%)
  between operations  15 us (7%)
  other arithmetic  8.94 us (4%)
  local copies, waits for them, and re-layouts  3.88 us (2%)
    pallas_call x3, Pallas kernels, call(): pl.pallas_call(body, grid=(KV_HEADS // PACK,), in_specs=[pl.BlockSpec(mem...  52 us
    ppermute x1, waiting for transfers between devices, scatter_last(): eighth = lax.ppermute(send, 'head', [(7, 6), (5, 4), (3, 2), (1, 0)])  26.3 us
    reduce_scatter x1, waiting for transfers between devices, per_device(): home = lax.psum_scatter(dnear, 'head', scatter_dimension=0)  25.1 us
    all_to_all x2, blocking collectives, swap(): return lax.all_to_all(pieces, axis, split_axis=0, concat_axis=0, tiled=True)  23 us
    all_to_all x4, starting transfers between devices, swap(): return lax.all_to_all(pieces, axis, split_axis=0, concat_axis=0, tiled=True)  21.2 us
    all_to_all x4, waiting for transfers between devices, swap(): return lax.all_to_all(pieces, axis, split_axis=0, concat_axis=0, tiled=True)  13.5 us
  transfers between devices with their start and end apart: 12, of which 6 were waited for; matrix products, arithmetic and copies ran while one was open for 4% of the time, Pallas kernels for 20%

profile of v4, /device:TPU:1, one launch (start us, length us, event | category | flops | bytes accessed | tf_op | source)
XLA Modules:
  0.0 199.8 jit_solution(5809786455376087268)
XLA Ops:
  7.2 0.0 copy-start.2
  7.2 0.0 copy-start.1
  7.2 0.0 all-gather.3.cloned.1.call-start
  7.2 1.9 pad_maximum_fusion
  9.1 0.0 all-gather.3.cloned.1.call-update
  9.1 1.0 slice.59
  10.1 0.7 collective-permute-start
  10.8 0.0 collective-permute-done
  10.8 1.0 slice_select_fusion
  11.8 0.7 collective-permute-start.1
  12.5 0.8 broadcast_compare_fusion
  13.3 0.0 collective-permute-done.1
  13.3 1.3 collective-permute-start.2
  14.6 26.3 %collective-permute-done.2 = bf16[2,16,1024]{2,1,0:T(8,128)(2,1)S(1)} collective-permute-done((bf16[2,16,1024]{2,1,0:T(8,128)(2,1)S(1)}, bf16[2,16,1024]{2,1,0:T(8,128)(2,1)S(1)}, u32[]{:S(2)}, u32[]{:S(2)}) %collective-permute-start.2) | collective-permute-done | bytes 65568 | tf_op jit(solution)/shard_map/ppermute | solution.py:261
  40.9 0.6 fusion.10
  41.6 10.3 %all-to-all-start = ((bf16[32,8,128]{2,1,0:T(8,128)(2,1)}), bf16[32,8,128]{2,1,0:T(8,128)(2,1)S(1)}, u32[]{:S(2)}, u32[]{:S(2)}) async-start(bf16[32,8,128]{2,1,0:T(8,128)(2,1)} %bitcast.5), calls=%async_computation | async-start | bytes 131072 | tf_op jit(solution)/shard_map/all_to_all | solution.py:246
  51.9 1.7 fusion.5.bias
  53.6 0.0 copy-done.2
  53.6 0.6 dynamic_slice.7
  54.8 4.3 %all-to-all-done = bf16[32,8,128]{2,1,0:T(8,128)(2,1)S(1)} async-done(((bf16[32,8,128]{2,1,0:T(8,128)(2,1)}), bf16[32,8,128]{2,1,0:T(8,128)(2,1)S(1)}, u32[]{:S(2)}, u32[]{:S(2)}) %all-to-all-start) | async-done | bytes 65568 | tf_op jit(solution)/shard_map/all_to_all | solution.py:246
  59.2 0.0 copy-done.1
  59.2 0.2 fusion
  59.4 0.7 copy.12
  60.0 3.9 %all-to-all-start.1 = ((bf16[32,8,128]{2,1,0:T(8,128)(2,1)}), bf16[32,8,128]{2,1,0:T(8,128)(2,1)S(1)}, u32[]{:S(2)}, u32[]{:S(2)}) async-start(bf16[32,8,128]{2,1,0:T(8,128)(2,1)} %bitcast.33), calls=%async_computation.1 | async-start | bytes 131072 | tf_op jit(solution)/shard_map/all_to_all | solution.py:246
  64.0 7.4 %all-to-all-done.1 = bf16[32,8,128]{2,1,0:T(8,128)(2,1)S(1)} async-done(((bf16[32,8,128]{2,1,0:T(8,128)(2,1)}), bf16[32,8,128]{2,1,0:T(8,128)(2,1)S(1)}, u32[]{:S(2)}, u32[]{:S(2)}) %all-to-all-start.1) | async-done | bytes 65568 | tf_op jit(solution)/shard_map/all_to_all | solution.py:246
  71.4 0.9 broadcast_in_dim.39
  72.2 3.5 %all-to-all-start.2 = ((bf16[8,2,16,1024]{3,2,1,0:T(8,128)(2,1)}), bf16[8,2,16,1024]{3,2,1,0:T(8,128)(2,1)S(1)}, u32[]{:S(2)}, u32[]{:S(2)}) async-start(bf16[8,2,16,1024]{3,2,1,0:T(8,128)(2,1)} %broadcast_in_dim.39), calls=%async_computation.2 | async-start | bytes 1048576 | tf_op jit(solution)/shard_map/all_to_all | solution.py:246
  75.7 0.7 and_select_fusion.bias
  76.5 0.0 all-gather.3.cloned.1.call-done
  76.5 15.4 %shard_map.102 = (f32[8,2,1024]{2,1,0:T(2,128)}, f32[8,128,1024]{2,1,0:T(8,128)}) custom-call(f32[1024,128]{1,0:T(8,128)} %fusion.5.bias, bf16[128,8192]{1,0:T(8,128)(2,1)} %q_ref.5, bf16[8,2,128,1024]{3,2,1,0:T(8,128)(2,1)} %bitcast.65), custom_call_target="tpu_custom_call" | custom-call | flops 8589934592 | bytes 16777216 | tf_op jit(solution)/shard_map/pallas_call | solution.py:192
  91.9 1.8 all-to-all-done.2.far
  93.7 0.0 copy-start
  93.7 0.8 copy-done
  94.5 12.1 %shard_map.103 = (bf16[128,8192]{1,0:T(8,128)(2,1)}, f32[8,2,1024]{2,1,0:T(2,128)}, f32[8,128,1024]{2,1,0:T(8,128)}, bf16[8,2,16,1024]{3,2,1,0:T(8,128)(2,1)}) custom-call(s32[1]{0:T(128)S(6)} %convert_element_type.38.flag, f32[128,128]{1,0:T(8,128)} %and_select_fusion.bias, bf16[128,8192]{1,0:T(8,128)(2,1)} %q_ref.5, bf16[128,8192]{1,0:T(8,128)(2,1)} %do_ref.3, ...), custom_call_target="tpu_custom_call" | custom-call | flops 6442450944 | bytes 16777216 | tf_op jit(solution)/shard_map/pallas_call | solution.py:192
  106.6 3.5 %all-to-all-start.3 = ((bf16[8,2,16,1024]{3,2,1,0:T(8,128)(2,1)}), bf16[8,2,16,1024]{3,2,1,0:T(8,128)(2,1)S(1)}, u32[]{:S(2)}, u32[]{:S(2)}) async-start(bf16[8,2,16,1024]{3,2,1,0:T(8,128)(2,1)} %get-tuple-element.21), calls=%async_computation.3 | async-start | bytes 1048576 | tf_op jit(solution)/shard_map/all_to_all | solution.py:246
  110.1 0.2 reduce-scatter.2.cloned.1.call-start
  110.3 24.5 %shard_map.104 = (bf16[128,8192]{1,0:T(8,128)(2,1)}, bf16[8,2,128,1024]{3,2,1,0:T(8,128)(2,1)}) custom-call(f32[1024,128]{1,0:T(8,128)} %fusion.5.bias, bf16[128,8192]{1,0:T(8,128)(2,1)} %q_ref.5, bf16[128,8192]{1,0:T(8,128)(2,1)} %do_ref.3, bf16[8,2,128,1024]{3,2,1,0:T(8,128)(2,1)} %bitcast.66, f32[8,2,1024]{2,1,0:T(2,128)} %get-tuple-element.17.stat, ...), custom_call_target="tpu_custom_call" | custom-call | flops 21474836480 | bytes 16777216 | tf_op jit(solution)/shard_map/pallas_call | solution.py:192
  134.8 0.0 all-to-all-done.3
  134.8 0.0 reduce-scatter.2.cloned.1.call-update
  134.8 0.1 reduce_sum.12
  134.9 12.1 %all_to_all.30 = bf16[32,8,128]{2,1,0:T(8,128)(2,1)S(1)} all-to-all(bf16[32,8,128]{2,1,0:T(8,128)(2,1)S(1)} %bitcast.63), channel_id=1, replica_groups=mesh['dp'=32,'head'=8] {'dp'}, dimensions={0} | all-to-all | bytes 131072 | tf_op jit(solution)/shard_map/all_to_all | solution.py:246
  147.0 0.3 fusion.1
  147.3 10.9 %all_to_all.31 = bf16[32,8,128]{2,1,0:T(8,128)(2,1)S(1)} all-to-all(bf16[32,8,128]{2,1,0:T(8,128)(2,1)S(1)} %bitcast.60), channel_id=1, replica_groups=mesh['dp'=32,'head'=8] {'dp'}, dimensions={0} | all-to-all | bytes 131072 | tf_op jit(solution)/shard_map/all_to_all | solution.py:246
  158.2 3.4 %collective-permute-start.3 = (bf16[2,16,1024]{2,1,0:T(8,128)(2,1)S(1)}, bf16[2,16,1024]{2,1,0:T(8,128)(2,1)S(1)}, u32[]{:S(2)}, u32[]{:S(2)}) collective-permute-start(bf16[2,16,1024]{2,1,0:T(8,128)(2,1)S(1)} %bitcast.53), channel_id=1, source_target_pairs={{0,1},{2,3},{4,5},{6,7},{8,9},{10,11},{12,13},{14,15},{16,17},{18,... | collective-permute-start | bytes 196616 | tf_op jit(solution)/shard_map/ppermute | solution.py:266
  161.6 2.8 %collective-permute-done.3 = bf16[2,16,1024]{2,1,0:T(8,128)(2,1)S(1)} collective-permute-done((bf16[2,16,1024]{2,1,0:T(8,128)(2,1)S(1)}, bf16[2,16,1024]{2,1,0:T(8,128)(2,1)S(1)}, u32[]{:S(2)}, u32[]{:S(2)}) %collective-permute-start.3) | collective-permute-done | bytes 65568 | tf_op jit(solution)/shard_map/ppermute | solution.py:266
  164.4 0.7 collective-permute-start.4
  165.1 0.0 collective-permute-done.4
  165.1 0.7 collective-permute-start.5
  165.8 0.0 collective-permute-done.5
  165.9 25.1 %reduce-scatter.2.cloned.1.call-done = bf16[1,2,128,1024]{3,2,1,0:T(8,128)(2,1)} async-done(((bf16[8,2,128,1024]{3,2,1,0:T(8,128)(2,1)}), bf16[1,2,128,1024]{3,2,1,0:T(8,128)(2,1)}) %reduce-scatter.2.cloned.1.call-update) | async-done | bytes 524304 | tf_op jit(solution)/shard_map/reduce_scatter | solution.py:300
  190.9 2.0 %fusion.2 = (bf16[128,1024]{1,0:T(8,128)(2,1)}, bf16[128,1024]{1,0:T(8,128)(2,1)}) fusion(bf16[2,128,1024]{2,1,0:T(8,128)(2,1)S(1)} %pad_maximum_fusion.1, bf16[1,2,128,1024]{3,2,1,0:T(8,128)(2,1)} %reduce-scatter.2.cloned.1.call-done, pred[]{:T(512)S(6)} %eq.63), kind=kLoop, calls=%fused_computation.7 | loop fusion | flops 1310720 | bytes 1572865 | tf_op jit(solution)/shard_map/convert_element_type | solution.py:304
  (9 shorter events, 0.1 us)
Async XLA Ops:
  7.2 46.4 %copy-start.2 = (s32[32]{0:T(128)S(1)}, s32[32]{0:T(128)}, u32[]{:S(2)}) copy-start(s32[32]{0:T(128)} %param.13) | copy-start | bytes 388
  7.2 52.0 %copy-start.1 = (s32[32]{0:T(128)S(1)}, s32[32]{0:T(128)}, u32[]{:S(2)}) copy-start(s32[32]{0:T(128)} %param.12) | copy-start | bytes 388
  7.2 69.3 %all-gather.3.cloned.1.call-start = ((), (), s32[]{:S(2)}) async-start(), calls=%async_computation.8 | async-start | bytes 4718592 | tf_op jit(solution)/shard_map/all_gather | solution.py:278
  10.1 0.7 collective-permute-start
  11.8 1.5 collective-permute-start.1
  13.3 27.6 %collective-permute-start.2 = (bf16[2,16,1024]{2,1,0:T(8,128)(2,1)S(1)}, bf16[2,16,1024]{2,1,0:T(8,128)(2,1)S(1)}, u32[]{:S(2)}, u32[]{:S(2)}) collective-permute-start(bf16[2,16,1024]{2,1,0:T(8,128)(2,1)S(1)} %slice_select_fusion.3), channel_id=1, source_target_pairs={{7,6},{5,4},{3,2},{1,0},{15,14},{13,12},{11,10},{9,8},{23,22},{21,... | collective-permute-start | bytes 196616 | tf_op jit(solution)/shard_map/ppermute | solution.py:261
  41.6 17.6 %all-to-all-start = ((bf16[32,8,128]{2,1,0:T(8,128)(2,1)}), bf16[32,8,128]{2,1,0:T(8,128)(2,1)S(1)}, u32[]{:S(2)}, u32[]{:S(2)}) async-start(bf16[32,8,128]{2,1,0:T(8,128)(2,1)} %bitcast.5), calls=%async_computation | async-start | bytes 131072 | tf_op jit(solution)/shard_map/all_to_all | solution.py:246
  60.0 11.3 %all-to-all-start.1 = ((bf16[32,8,128]{2,1,0:T(8,128)(2,1)}), bf16[32,8,128]{2,1,0:T(8,128)(2,1)S(1)}, u32[]{:S(2)}, u32[]{:S(2)}) async-start(bf16[32,8,128]{2,1,0:T(8,128)(2,1)} %bitcast.33), calls=%async_computation.1 | async-start | bytes 131072 | tf_op jit(solution)/shard_map/all_to_all | solution.py:246
  72.2 21.4 %all-to-all-start.2 = ((bf16[8,2,16,1024]{3,2,1,0:T(8,128)(2,1)}), bf16[8,2,16,1024]{3,2,1,0:T(8,128)(2,1)S(1)}, u32[]{:S(2)}, u32[]{:S(2)}) async-start(bf16[8,2,16,1024]{3,2,1,0:T(8,128)(2,1)} %broadcast_in_dim.39), calls=%async_computation.2 | async-start | bytes 1048576 | tf_op jit(solution)/shard_map/all_to_all | solution.py:246
  93.7 0.8 copy-start
  106.6 28.2 %all-to-all-start.3 = ((bf16[8,2,16,1024]{3,2,1,0:T(8,128)(2,1)}), bf16[8,2,16,1024]{3,2,1,0:T(8,128)(2,1)S(1)}, u32[]{:S(2)}, u32[]{:S(2)}) async-start(bf16[8,2,16,1024]{3,2,1,0:T(8,128)(2,1)} %get-tuple-element.21), calls=%async_computation.3 | async-start | bytes 1048576 | tf_op jit(solution)/shard_map/all_to_all | solution.py:246
  110.1 80.9 %reduce-scatter.2.cloned.1.call-start = ((), (), s32[]{:S(2)}) async-start(), calls=%async_computation.7 | async-start | bytes 4718592 | tf_op jit(solution)/shard_map/reduce_scatter | solution.py:300
  158.2 6.2 %collective-permute-start.3 = (bf16[2,16,1024]{2,1,0:T(8,128)(2,1)S(1)}, bf16[2,16,1024]{2,1,0:T(8,128)(2,1)S(1)}, u32[]{:S(2)}, u32[]{:S(2)}) collective-permute-start(bf16[2,16,1024]{2,1,0:T(8,128)(2,1)S(1)} %bitcast.53), channel_id=1, source_target_pairs={{0,1},{2,3},{4,5},{6,7},{8,9},{10,11},{12,13},{14,15},{16,17},{18,... | collective-permute-start | bytes 196616 | tf_op jit(solution)/shard_map/ppermute | solution.py:266
  164.4 0.7 collective-permute-start.4
  165.1 0.7 collective-permute-start.5
Sparse Core Ops, SparseCore 0:
  10.4 58.8 all-gather.2
  135.0 55.9 reduce-scatter.1

commit v5 on v4

--- a/solution.py
+++ b/solution.py
@@ -253,22 +253,17 @@
 
 
 def scatter_last(kv, z):
-    half = lax.ppermute(kv[:, :64], "head", [(7, 3)])
-    mine = jnp.where(z == 7, kv[:, 64:], half)
-    send = jnp.where(z == 7, mine[:, :32], half[:, :32])
-    quarter = lax.ppermute(send, "head", [(7, 5), (3, 1)])
-    send = jnp.where(z % 4 == 3, mine[:, 32:48], quarter[:, :16])
-    eighth = lax.ppermute(send, "head", [(7, 6), (5, 4), (3, 2), (1, 0)])
-    return jnp.where(z % 2 == 0, eighth, jnp.where(z % 4 == 1, quarter[:, 16:], mine[:, 48:]))
+    parts = [lax.ppermute(kv[:, 32 * i : 32 * i + 32], "head", [(7, 2 * i + 1)]) for i in range(3)]
+    two = jnp.where(z == 7, kv[:, 96:], jnp.where(z == 1, parts[0], jnp.where(z == 3, parts[1], parts[2])))
+    even = lax.ppermute(two[:, :16], "head", [(i + 1, i) for i in (0, 2, 4, 6)])
+    return jnp.where(z % 2 == 0, even, two[:, 16:])
 
 
 def collect_last(piece):
-    two = lax.ppermute(piece, "head", [(i, i + 1) for i in (0, 2, 4, 6)])
-    two = jnp.concatenate([two, piece], axis=1)
-    four = lax.ppermute(two, "head", [(1, 3), (5, 7)])
-    four = jnp.concatenate([four, two], axis=1)
-    eight = lax.ppermute(four, "head", [(3, 7)])
-    return jnp.concatenate([eight, four], axis=1)
+    even = lax.ppermute(piece, "head", [(i, i + 1) for i in (0, 2, 4, 6)])
+    two = jnp.concatenate([even, piece], axis=1)
+    parts = [lax.ppermute(two, "head", [(i, 7)]) for i in (1, 3, 5)]
+    return jnp.concatenate([*parts, two], axis=1)
 
 
 def per_device(queries, input_keys, input_values, output_gradient, doc_ids, spill_src, spill_len):

time: 202 us -> 200 us (0.990)
  waiting for transfers between devices: 67.8 us -> 58.7 us
  blocking collectives: 23 us -> 30.3 us
    ppermute x6 -> x8, waiting for transfers between devices: 29.1 us -> 19.7 us  [the longest x1 16.9 us: scatter_last(): even = lax.ppermute(two[:, :16], 'head', [(i + 1, i) for i in (0, 2, 4, 6)])]
    all_to_all x2, blocking collectives: 23 us -> 30.3 us  [swap(): return lax.all_to_all(pieces, axis, split_axis=0, concat_axis=0, tiled=True)]
    all_to_all x4, waiting for transfers between devices: 13.5 us -> 11.2 us  [swap(): return lax.all_to_all(pieces, axis, split_axis=0, concat_axis=0, tiled=True)]
    ppermute x6 -> x8, starting transfers between devices: 7.41 us -> 8.61 us  [the longest x1 3.3 us: collect_last(): even = lax.ppermute(piece, 'head', [(i, i + 1) for i in (0, 2, 4, 6)])]
  transfers between devices with their start and end apart: 12 -> 14, of which waited for: 6 -> 7; matrix products, arithmetic and copies ran while one was open for 4% -> 5% of each run, Pallas kernels for 20% -> 20%
where the time goes in v5:
time: 200 us; the launch traced here: 199 us
  waiting for transfers between devices  58.7 us (29%)
  Pallas kernels  52 us (26%)
  blocking collectives  30.3 us (15%)
  starting transfers between devices  28.9 us (14%)
  between operations  15 us (8%)
  other arithmetic  8.79 us (4%)
  local copies, waits for them, and re-layouts  4.67 us (2%)
    pallas_call x3, Pallas kernels, call(): pl.pallas_call(body, grid=(KV_HEADS // PACK,), in_specs=[pl.BlockSpec(mem...  52 us
    all_to_all x2, blocking collectives, swap(): return lax.all_to_all(pieces, axis, split_axis=0, concat_axis=0, tiled=True)  30.3 us
    reduce_scatter x1, waiting for transfers between devices, per_device(): home = lax.psum_scatter(dnear, 'head', scatter_dimension=0)  26.1 us
    all_to_all x4, starting transfers between devices, swap(): return lax.all_to_all(pieces, axis, split_axis=0, concat_axis=0, tiled=True)  20 us
    ppermute x1, waiting for transfers between devices, scatter_last(): even = lax.ppermute(two[:, :16], 'head', [(i + 1, i) for i in (0, 2, 4, 6)])  16.9 us
    all_to_all x4, waiting for transfers between devices, swap(): return lax.all_to_all(pieces, axis, split_axis=0, concat_axis=0, tiled=True)  11.2 us
  transfers between devices with their start and end apart: 14, of which 7 were waited for; matrix products, arithmetic and copies ran while one was open for 5% of the time, Pallas kernels for 20%

profile of v5, /device:TPU:1, one launch (start us, length us, event | category | flops | bytes accessed | tf_op | source)
XLA Modules:
  0.0 199.5 jit_solution(16761029900471806698)
XLA Ops:
  7.2 0.0 all-gather.3.cloned.1.call-start
  7.2 1.9 pad_maximum_fusion
  9.1 0.0 all-gather.3.cloned.1.call-update
  9.1 1.1 fusion.12
  10.2 0.7 collective-permute-start.2
  10.9 0.7 collective-permute-start.1
  11.5 0.7 collective-permute-start
  12.2 0.8 broadcast_compare_fusion
  13.0 0.0 collective-permute-done.2
  13.0 0.0 collective-permute-done.1
  13.0 0.0 collective-permute-done
  13.0 0.9 slice_select_fusion
  14.0 1.3 collective-permute-start.3
  15.3 16.9 %collective-permute-done.3 = bf16[2,16,1024]{2,1,0:T(8,128)(2,1)S(1)} collective-permute-done((bf16[2,16,1024]{2,1,0:T(8,128)(2,1)S(1)}, bf16[2,16,1024]{2,1,0:T(8,128)(2,1)S(1)}, u32[]{:S(2)}, u32[]{:S(2)}) %collective-permute-start.3) | collective-permute-done | bytes 65568 | tf_op jit(solution)/shard_map/ppermute | solution.py:258
  32.1 0.6 slice_select_fusion.1
  32.8 9.1 %all-to-all-start = ((bf16[32,8,128]{2,1,0:T(8,128)(2,1)}), bf16[32,8,128]{2,1,0:T(8,128)(2,1)S(1)}, u32[]{:S(2)}, u32[]{:S(2)}) async-start(bf16[32,8,128]{2,1,0:T(8,128)(2,1)} %bitcast.5), calls=%async_computation | async-start | bytes 131072 | tf_op jit(solution)/shard_map/all_to_all | solution.py:246
  41.9 1.7 fusion.5.bias
  43.6 1.2 dynamic_slice.7
  45.5 3.7 %all-to-all-done = bf16[32,8,128]{2,1,0:T(8,128)(2,1)S(1)} async-done(((bf16[32,8,128]{2,1,0:T(8,128)(2,1)}), bf16[32,8,128]{2,1,0:T(8,128)(2,1)S(1)}, u32[]{:S(2)}, u32[]{:S(2)}) %all-to-all-start) | async-done | bytes 65568 | tf_op jit(solution)/shard_map/all_to_all | solution.py:246
  49.2 0.9 fusion
  50.0 0.6 copy.12
  50.7 3.9 %all-to-all-start.1 = ((bf16[32,8,128]{2,1,0:T(8,128)(2,1)}), bf16[32,8,128]{2,1,0:T(8,128)(2,1)S(1)}, u32[]{:S(2)}, u32[]{:S(2)}) async-start(bf16[32,8,128]{2,1,0:T(8,128)(2,1)} %bitcast.33), calls=%async_computation.1 | async-start | bytes 131072 | tf_op jit(solution)/shard_map/all_to_all | solution.py:246
  54.6 7.4 %all-to-all-done.1 = bf16[32,8,128]{2,1,0:T(8,128)(2,1)S(1)} async-done(((bf16[32,8,128]{2,1,0:T(8,128)(2,1)}), bf16[32,8,128]{2,1,0:T(8,128)(2,1)S(1)}, u32[]{:S(2)}, u32[]{:S(2)}) %all-to-all-start.1) | async-done | bytes 65568 | tf_op jit(solution)/shard_map/all_to_all | solution.py:246
  62.0 0.9 broadcast_in_dim.39
  62.9 3.6 %all-to-all-start.2 = ((bf16[8,2,16,1024]{3,2,1,0:T(8,128)(2,1)}), bf16[8,2,16,1024]{3,2,1,0:T(8,128)(2,1)S(1)}, u32[]{:S(2)}, u32[]{:S(2)}) async-start(bf16[8,2,16,1024]{3,2,1,0:T(8,128)(2,1)} %broadcast_in_dim.39), calls=%async_computation.2 | async-start | bytes 1048576 | tf_op jit(solution)/shard_map/all_to_all | solution.py:246
  66.5 0.7 and_select_fusion.bias
  67.2 1.8 all-gather.3.cloned.1.call-done
  69.0 15.3 %shard_map.102 = (f32[8,2,1024]{2,1,0:T(2,128)}, f32[8,128,1024]{2,1,0:T(8,128)}) custom-call(f32[1024,128]{1,0:T(8,128)} %fusion.5.bias, bf16[128,8192]{1,0:T(8,128)(2,1)} %q_ref.5, bf16[8,2,128,1024]{3,2,1,0:T(8,128)(2,1)} %bitcast.66), custom_call_target="tpu_custom_call" | custom-call | flops 8589934592 | bytes 16777216 | tf_op jit(solution)/shard_map/pallas_call | solution.py:192
  84.4 0.1 all-to-all-done.2.far
  84.4 0.0 copy-start
  84.4 0.8 copy-done
  85.2 12.1 %shard_map.103 = (bf16[128,8192]{1,0:T(8,128)(2,1)}, f32[8,2,1024]{2,1,0:T(2,128)}, f32[8,128,1024]{2,1,0:T(8,128)}, bf16[8,2,16,1024]{3,2,1,0:T(8,128)(2,1)}) custom-call(s32[1]{0:T(128)S(6)} %convert_element_type.38.flag, f32[128,128]{1,0:T(8,128)} %and_select_fusion.bias, bf16[128,8192]{1,0:T(8,128)(2,1)} %q_ref.5, bf16[128,8192]{1,0:T(8,128)(2,1)} %do_ref.3, ...), custom_call_target="tpu_custom_call" | custom-call | flops 6442450944 | bytes 16777216 | tf_op jit(solution)/shard_map/pallas_call | solution.py:192
  97.3 3.5 %all-to-all-start.3 = ((bf16[8,2,16,1024]{3,2,1,0:T(8,128)(2,1)}), bf16[8,2,16,1024]{3,2,1,0:T(8,128)(2,1)S(1)}, u32[]{:S(2)}, u32[]{:S(2)}) async-start(bf16[8,2,16,1024]{3,2,1,0:T(8,128)(2,1)} %get-tuple-element.21), calls=%async_computation.3 | async-start | bytes 1048576 | tf_op jit(solution)/shard_map/all_to_all | solution.py:246
  100.8 0.2 reduce-scatter.2.cloned.1.call-start
  101.1 24.5 %shard_map.104 = (bf16[128,8192]{1,0:T(8,128)(2,1)}, bf16[8,2,128,1024]{3,2,1,0:T(8,128)(2,1)}) custom-call(f32[1024,128]{1,0:T(8,128)} %fusion.5.bias, bf16[128,8192]{1,0:T(8,128)(2,1)} %q_ref.5, bf16[128,8192]{1,0:T(8,128)(2,1)} %do_ref.3, bf16[8,2,128,1024]{3,2,1,0:T(8,128)(2,1)} %bitcast.67, f32[8,2,1024]{2,1,0:T(2,128)} %get-tuple-element.17.stat, ...), custom_call_target="tpu_custom_call" | custom-call | flops 21474836480 | bytes 16777216 | tf_op jit(solution)/shard_map/pallas_call | solution.py:192
  125.6 0.0 copy-start.1
  125.6 0.0 all-to-all-done.3
  125.6 0.0 reduce-scatter.2.cloned.1.call-update
  125.6 0.1 reduce_sum.12
  125.7 19.4 %all_to_all.30 = bf16[32,8,128]{2,1,0:T(8,128)(2,1)S(1)} all-to-all(bf16[32,8,128]{2,1,0:T(8,128)(2,1)S(1)} %bitcast.64), channel_id=1, replica_groups=mesh['dp'=32,'head'=8] {'dp'}, dimensions={0} | all-to-all | bytes 131072 | tf_op jit(solution)/shard_map/all_to_all | solution.py:246
  145.1 0.0 copy-done.1
  145.1 0.3 fusion.1
  145.4 10.9 %all_to_all.31 = bf16[32,8,128]{2,1,0:T(8,128)(2,1)S(1)} all-to-all(bf16[32,8,128]{2,1,0:T(8,128)(2,1)S(1)} %bitcast.61), channel_id=1, replica_groups=mesh['dp'=32,'head'=8] {'dp'}, dimensions={0} | all-to-all | bytes 131072 | tf_op jit(solution)/shard_map/all_to_all | solution.py:246
  156.3 3.3 %collective-permute-start.4 = (bf16[2,16,1024]{2,1,0:T(8,128)(2,1)S(1)}, bf16[2,16,1024]{2,1,0:T(8,128)(2,1)S(1)}, u32[]{:S(2)}, u32[]{:S(2)}) collective-permute-start(bf16[2,16,1024]{2,1,0:T(8,128)(2,1)S(1)} %bitcast.55), channel_id=1, source_target_pairs={{0,1},{2,3},{4,5},{6,7},{8,9},{10,11},{12,13},{14,15},{16,17},{18,... | collective-permute-start | bytes 196616 | tf_op jit(solution)/shard_map/ppermute | solution.py:263
  159.6 2.8 %collective-permute-done.4 = bf16[2,16,1024]{2,1,0:T(8,128)(2,1)S(1)} collective-permute-done((bf16[2,16,1024]{2,1,0:T(8,128)(2,1)S(1)}, bf16[2,16,1024]{2,1,0:T(8,128)(2,1)S(1)}, u32[]{:S(2)}, u32[]{:S(2)}) %collective-permute-start.4) | collective-permute-done | bytes 65568 | tf_op jit(solution)/shard_map/ppermute | solution.py:263
  162.4 0.7 collective-permute-start.5
  163.1 0.7 collective-permute-start.6
  163.8 0.7 collective-permute-start.7
  164.4 0.0 collective-permute-done.5
  164.5 0.0 collective-permute-done.6
  164.5 0.0 collective-permute-done.7
  164.6 26.1 %reduce-scatter.2.cloned.1.call-done = bf16[1,2,128,1024]{3,2,1,0:T(8,128)(2,1)} async-done(((bf16[8,2,128,1024]{3,2,1,0:T(8,128)(2,1)}), bf16[1,2,128,1024]{3,2,1,0:T(8,128)(2,1)}) %reduce-scatter.2.cloned.1.call-update) | async-done | bytes 524304 | tf_op jit(solution)/shard_map/reduce_scatter | solution.py:295
  190.6 2.0 %fusion.2 = (bf16[128,1024]{1,0:T(8,128)(2,1)}, bf16[128,1024]{1,0:T(8,128)(2,1)}) fusion(bf16[2,128,1024]{2,1,0:T(8,128)(2,1)S(1)} %constant_dynamic-update-slice_fusion, bf16[1,2,128,1024]{3,2,1,0:T(8,128)(2,1)} %reduce-scatter.2.cloned.1.call-done, pred[]{:T(512)S(6)} %eq.59), kind=kLoop, calls=%fused_computation.6 | loop fusion | flops 1310720 | bytes 1572865 | tf_op jit(solution)/shard_map/convert_element_type | solution.py:299
  (11 shorter events, 0.1 us)
Async XLA Ops:
  7.2 61.8 %all-gather.3.cloned.1.call-start = ((), (), s32[]{:S(2)}) async-start(), calls=%async_computation.8 | async-start | bytes 4718592 | tf_op jit(solution)/shard_map/all_gather | solution.py:273
  10.2 2.8 %collective-permute-start.2 = (bf16[2,32,1024]{2,1,0:T(8,128)(2,1)S(1)}, bf16[2,32,1024]{2,1,0:T(8,128)(2,1)S(1)}, u32[]{:S(2)}, u32[]{:S(2)}) collective-permute-start(bf16[2,32,1024]{2,1,0:T(8,128)(2,1)S(1)} %get-tuple-element.28), channel_id=1, source_target_pairs={{7,5},{15,13},{23,21},{31,29},{39,37},{47,45},{55,53},{63,61},{71,... | collective-permute-start | bytes 393224 | tf_op jit(solution)/shard_map/ppermute | solution.py:256
  10.9 2.1 %collective-permute-start.1 = (bf16[2,32,1024]{2,1,0:T(8,128)(2,1)S(1)}, bf16[2,32,1024]{2,1,0:T(8,128)(2,1)S(1)}, u32[]{:S(2)}, u32[]{:S(2)}) collective-permute-start(bf16[2,32,1024]{2,1,0:T(8,128)(2,1)S(1)} %get-tuple-element.29), channel_id=1, source_target_pairs={{7,3},{15,11},{23,19},{31,27},{39,35},{47,43},{55,51},{63,59},{71,... | collective-permute-start | bytes 393224 | tf_op jit(solution)/shard_map/ppermute | solution.py:256
  11.5 1.5 collective-permute-start
  14.0 18.2 %collective-permute-start.3 = (bf16[2,16,1024]{2,1,0:T(8,128)(2,1)S(1)}, bf16[2,16,1024]{2,1,0:T(8,128)(2,1)S(1)}, u32[]{:S(2)}, u32[]{:S(2)}) collective-permute-start(bf16[2,16,1024]{2,1,0:T(8,128)(2,1)S(1)} %slice.54), channel_id=1, source_target_pairs={{1,0},{3,2},{5,4},{7,6},{9,8},{11,10},{13,12},{15,14},{17,16},{19,... | collective-permute-start | bytes 196616 | tf_op jit(solution)/shard_map/ppermute | solution.py:258
  32.8 16.4 %all-to-all-start = ((bf16[32,8,128]{2,1,0:T(8,128)(2,1)}), bf16[32,8,128]{2,1,0:T(8,128)(2,1)S(1)}, u32[]{:S(2)}, u32[]{:S(2)}) async-start(bf16[32,8,128]{2,1,0:T(8,128)(2,1)} %bitcast.5), calls=%async_computation | async-start | bytes 131072 | tf_op jit(solution)/shard_map/all_to_all | solution.py:246
  50.7 11.3 %all-to-all-start.1 = ((bf16[32,8,128]{2,1,0:T(8,128)(2,1)}), bf16[32,8,128]{2,1,0:T(8,128)(2,1)S(1)}, u32[]{:S(2)}, u32[]{:S(2)}) async-start(bf16[32,8,128]{2,1,0:T(8,128)(2,1)} %bitcast.33), calls=%async_computation.1 | async-start | bytes 131072 | tf_op jit(solution)/shard_map/all_to_all | solution.py:246
  62.9 21.5 %all-to-all-start.2 = ((bf16[8,2,16,1024]{3,2,1,0:T(8,128)(2,1)}), bf16[8,2,16,1024]{3,2,1,0:T(8,128)(2,1)S(1)}, u32[]{:S(2)}, u32[]{:S(2)}) async-start(bf16[8,2,16,1024]{3,2,1,0:T(8,128)(2,1)} %broadcast_in_dim.39), calls=%async_computation.2 | async-start | bytes 1048576 | tf_op jit(solution)/shard_map/all_to_all | solution.py:246
  84.4 0.8 copy-start
  97.3 28.2 %all-to-all-start.3 = ((bf16[8,2,16,1024]{3,2,1,0:T(8,128)(2,1)}), bf16[8,2,16,1024]{3,2,1,0:T(8,128)(2,1)S(1)}, u32[]{:S(2)}, u32[]{:S(2)}) async-start(bf16[8,2,16,1024]{3,2,1,0:T(8,128)(2,1)} %get-tuple-element.21), calls=%async_computation.3 | async-start | bytes 1048576 | tf_op jit(solution)/shard_map/all_to_all | solution.py:246
  100.8 89.8 %reduce-scatter.2.cloned.1.call-start = ((), (), s32[]{:S(2)}) async-start(), calls=%async_computation.7 | async-start | bytes 4718592 | tf_op jit(solution)/shard_map/reduce_scatter | solution.py:295
  125.6 19.5 %copy-start.1 = (s32[32]{0:T(128)S(1)}, s32[32]{0:T(128)}, u32[]{:S(2)}) copy-start(s32[32]{0:T(128)} %param.12) | copy-start | bytes 388
  156.3 6.1 %collective-permute-start.4 = (bf16[2,16,1024]{2,1,0:T(8,128)(2,1)S(1)}, bf16[2,16,1024]{2,1,0:T(8,128)(2,1)S(1)}, u32[]{:S(2)}, u32[]{:S(2)}) collective-permute-start(bf16[2,16,1024]{2,1,0:T(8,128)(2,1)S(1)} %bitcast.55), channel_id=1, source_target_pairs={{0,1},{2,3},{4,5},{6,7},{8,9},{10,11},{12,13},{14,15},{16,17},{18,... | collective-permute-start | bytes 196616 | tf_op jit(solution)/shard_map/ppermute | solution.py:263
  162.4 2.0 %collective-permute-start.5 = (bf16[2,32,1024]{2,1,0:T(8,128)(2,1)S(1)}, bf16[2,32,1024]{2,1,0:T(8,128)(2,1)S(1)}, u32[]{:S(2)}, u32[]{:S(2)}) collective-permute-start(bf16[2,32,1024]{2,1,0:T(8,128)(2,1)S(1)} %pad_maximum_fusion.1), channel_id=1, source_target_pairs={{1,7},{9,15},{17,23},{25,31},{33,39},{41,47},{49,55},{57,63},{65,7... | collective-permute-start | bytes 393224 | tf_op jit(solution)/shard_map/ppermute | solution.py:265
  163.1 1.4 collective-permute-start.6
  163.8 0.7 collective-permute-start.7
Sparse Core Ops, SparseCore 0:
  10.4 58.6 all-gather.2
  125.7 64.8 reduce-scatter.1
